TPU v7x, 512 devices: a whole 4x8x8 slice. The times are simulated.
512 devices in a mesh: gx: 8 (over z_lo, core), gy: 8 (over x, z_hi), gz: 8 (over y).
Axes of the slice: x: 4, y: 8, z: 8 (z_hi: 2, z_lo: 4; z = z_hi * 4 + z_lo), core: 2. Of those that a mesh axis runs over, the one named last changes fastest.
Arguments:
- tokens: bfloat16 [1024, 8192], P('gx', ('gz', 'gy')), may hold values from -6 to 6
- gate_weight: bfloat16 [8192, 16384], P('gz', ('gy', 'gx')), may hold values from -0.0625 to 0.0625
- up_weight: bfloat16 [8192, 16384], P('gz', ('gy', 'gx')), may hold values from -0.0625 to 0.0625
- hidden_grad: bfloat16 [1024, 16384], P('gx', ('gy', 'gz')), may hold values from -1.5 to 1.5
Outputs:
- hidden: bfloat16 [1024, 16384], P('gx', ('gy', 'gz'))
- input_grad: bfloat16 [1024, 8192], P('gx', ('gz', 'gy'))
- gate_wgrad: bfloat16 [8192, 16384], P('gz', ('gy', 'gx'))
- up_wgrad: bfloat16 [8192, 16384], P('gz', ('gy', 'gx'))
All inputs are finite; a program needn't handle non-finite values.
Results may differ from a plain program's by a relative error of at most 0.005.
Values may be sent and summed in bfloat16 or wider, within the bound.
No kernel may reach another device: no remote copies, remote signals or barrier semaphores. Data moves between devices by JAX's collectives and lax.ppermute only.
A program may use at most 64 MiB of HBM per device.

v0:
```python
import jax
import jax.numpy as jnp
from jax import lax
from jax.sharding import PartitionSpec as P


def fetch_blocks(gate_weight, up_weight):
    return (
        lax.all_gather(gate_weight, "gx", axis=1, tiled=True),
        lax.all_gather(up_weight, "gx", axis=1, tiled=True),
    )


def body(tokens, gate_weight, up_weight, hidden_grad):
    contract_last = (((1,), (1,)), ((), ()))
    contract_rows = (((0,), (0,)), ((), ()))
    block_rows = lax.all_gather(tokens, "gy", axis=1, tiled=True)
    all_rows = lax.all_gather(block_rows, "gx", axis=0, tiled=True)
    gate_block, up_block = fetch_blocks(gate_weight, up_weight)
    gate_part = jnp.dot(block_rows, gate_block, preferred_element_type=jnp.float32)
    up_part = jnp.dot(block_rows, up_block, preferred_element_type=jnp.float32)
    gate_sum, up_sum = (
        lax.psum_scatter(gate_part, "gz", scatter_dimension=1, tiled=True),
        lax.psum_scatter(up_part, "gz", scatter_dimension=1, tiled=True),
    )
    sigmoid_gate = jax.nn.sigmoid(gate_sum)
    activated = gate_sum * sigmoid_gate
    hidden = (activated * up_sum).astype(jnp.bfloat16)
    upstream = hidden_grad.astype(jnp.float32)
    gate_grad = (upstream * up_sum * sigmoid_gate * (1.0 + gate_sum * (1.0 - sigmoid_gate))).astype(
        jnp.bfloat16
    )
    up_grad = (upstream * activated).astype(jnp.bfloat16)
    gate_wide, up_wide = (
        lax.all_gather(gate_grad, "gz", axis=1, tiled=True),
        lax.all_gather(up_grad, "gz", axis=1, tiled=True),
    )
    gate_tall, up_tall = (
        lax.all_to_all(gate_wide, "gx", split_axis=1, concat_axis=0, tiled=True),
        lax.all_to_all(up_wide, "gx", split_axis=1, concat_axis=0, tiled=True),
    )
    gate_wgrad = lax.dot_general(
        all_rows, gate_tall, contract_rows, preferred_element_type=jnp.float32
    )
    up_wgrad = lax.dot_general(all_rows, up_tall, contract_rows, preferred_element_type=jnp.float32)
    input_part = lax.dot_general(
        gate_wide, gate_block, contract_last, preferred_element_type=jnp.float32
    )
    input_part = input_part + lax.dot_general(
        up_wide, up_block, contract_last, preferred_element_type=jnp.float32
    )
    input_grad = lax.psum_scatter(input_part, "gy", scatter_dimension=1, tiled=True)
    return (
        hidden,
        input_grad.astype(jnp.bfloat16),
        gate_wgrad.astype(jnp.bfloat16),
        up_wgrad.astype(jnp.bfloat16),
    )


def solution(mesh):
    in_specs = (
        P("gx", ("gz", "gy")),
        P("gz", ("gy", "gx")),
        P("gz", ("gy", "gx")),
        P("gx", ("gy", "gz")),
    )
    out_specs = (
        P("gx", ("gy", "gz")),
        P("gx", ("gz", "gy")),
        P("gz", ("gy", "gx")),
        P("gz", ("gy", "gx")),
    )
    return jax.shard_map(body, mesh=mesh, in_specs=in_specs, out_specs=out_specs, check_vma=False)
```

profile of v0, /device:TPU:6, one launch (start us, length us, event | category | flops | bytes accessed | tf_op | source)
XLA Modules:
  0.0 391.4 jit_solution(14217261124911969666)
XLA Ops:
  7.2 0.0 all-gather.4.cloned.1.call-start
  7.2 0.7 all-gather.4.cloned.1.call-update
  7.9 0.0 all-gather.6.cloned.1.call-start
  7.9 0.7 all-gather.6.cloned.1.call-update
  8.6 0.0 reduce-scatter.4.cloned.1.call-start
  8.7 45.3 %all_gather.18 = bf16[128,1024]{1,0:T(8,128)(2,1)S(1)} all-gather(bf16[128,128]{1,0:T(8,128)(2,1)} %param.4), channel_id=1, replica_groups=mesh['gx'=8,'gy'=8,'gz'=8] {'gy'}, dimensions={1}, use_global_device_ids=true | all-gather | bytes 294912 | tf_op jit(solution)/shard_map/all_gather | solution.py:17
  54.0 22.2 %all-gather.4.cloned.1.call-done = bf16[1024,2048]{1,0:T(8,128)(2,1)} async-done(((bf16[1024,256]{1,0:T(8,128)(2,1)}), bf16[1024,2048]{1,0:T(8,128)(2,1)}) %all-gather.4.cloned.1.call-update) | async-done | bytes 4194320 | tf_op jit(solution)/shard_map/all_gather | solution.py:9
  76.3 3.9 fusion.7
  80.2 0.0 reduce-scatter.6.cloned.1.call-start
  80.2 54.7 %all-gather.6.cloned.1.call-done = bf16[1024,2048]{1,0:T(8,128)(2,1)} async-done(((bf16[1024,256]{1,0:T(8,128)(2,1)}), bf16[1024,2048]{1,0:T(8,128)(2,1)}) %all-gather.6.cloned.1.call-update) | async-done | bytes 4194320 | tf_op jit(solution)/shard_map/all_gather | solution.py:10
  134.9 3.9 fusion.8
  138.9 0.0 all-gather.8.cloned.1.call-start
  138.9 0.5 all-gather.8.cloned.1.call-update
  139.5 39.7 %reduce-scatter.4.cloned.1.call-done = f32[128,256]{1,0:T(8,128)} async-done(((f32[128,2048]{1,0:T(8,128)}), f32[128,256]{1,0:T(8,128)}) %reduce-scatter.4.cloned.1.call-update) | async-done | bytes 131088 | tf_op jit(solution)/shard_map/reduce_scatter | solution.py:23
  179.2 42.9 %reduce-scatter.6.cloned.1.call-done = f32[128,256]{1,0:T(8,128)} async-done(((f32[128,2048]{1,0:T(8,128)}), f32[128,256]{1,0:T(8,128)}) %reduce-scatter.6.cloned.1.call-update) | async-done | bytes 131088 | tf_op jit(solution)/shard_map/reduce_scatter | solution.py:24
  222.1 1.7 fusion.4
  223.8 25.5 %all_gather.21 = bf16[128,2048]{1,0:T(8,128)(2,1)S(1)} all-gather(bf16[128,256]{1,0:T(8,128)(2,1)S(1)} %get-tuple-element.12), channel_id=1, replica_groups=mesh['gx'=8,'gy'=8,'gz'=8] {'gz'}, dimensions={1}, use_global_device_ids=true | all-gather | bytes 589824 | tf_op jit(solution)/shard_map/all_gather | solution.py:35
  249.3 0.8 copy.19
  250.1 5.1 %all-to-all-start = ((bf16[128,8,256]{2,0,1:T(8,128)(2,1)}), bf16[128,8,256]{2,0,1:T(8,128)(2,1)S(1)}, u32[]{:S(2)}, u32[]{:S(2)}) async-start(bf16[128,8,256]{2,0,1:T(8,128)(2,1)} %bitcast.29), calls=%async_computation.3 | async-start | bytes 1048576 | tf_op jit(solution)/shard_map/all_to_all | solution.py:39
  255.2 25.5 %all_gather.22 = bf16[128,2048]{1,0:T(8,128)(2,1)S(1)} all-gather(bf16[128,256]{1,0:T(8,128)(2,1)S(1)} %get-tuple-element.14), channel_id=1, replica_groups=mesh['gx'=8,'gy'=8,'gz'=8] {'gz'}, dimensions={1}, use_global_device_ids=true | all-gather | bytes 589824 | tf_op jit(solution)/shard_map/all_gather | solution.py:36
  280.7 0.8 copy.18
  281.5 3.7 fusion.9
  285.2 5.0 %all-to-all-start.1 = ((bf16[128,8,256]{2,0,1:T(8,128)(2,1)}), bf16[128,8,256]{2,0,1:T(8,128)(2,1)S(1)}, u32[]{:S(2)}, u32[]{:S(2)}) async-start(bf16[128,8,256]{2,0,1:T(8,128)(2,1)} %bitcast.28), calls=%async_computation.4 | async-start | bytes 1048576 | tf_op jit(solution)/shard_map/all_to_all | solution.py:40
  290.2 0.0 reduce-scatter.8.cloned.1.call-start
  290.2 4.5 %convolution_add_fusion = f32[128,1024]{1,0:T(8,128)} fusion(f32[128,1024]{1,0:T(8,128)S(1)} %fusion.9, bf16[128,2048]{1,0:T(8,128)(2,1)S(1)} %all_gather.22, bf16[1024,2048]{1,0:T(8,128)(2,1)} %all-gather.6.cloned.1.call-done), kind=kOutput, calls=%fused_computation.2 | convolution fusion | flops 537001984 | bytes 5767168 | tf_op jit(solution)/shard_map/dot_general | solution.py:49
  294.8 3.3 fusion
  298.1 2.0 copy.12
  300.1 5.4 %all-to-all-done.1 = bf16[128,8,256]{2,0,1:T(8,128)(2,1)S(1)} async-done(((bf16[128,8,256]{2,0,1:T(8,128)(2,1)}), bf16[128,8,256]{2,0,1:T(8,128)(2,1)S(1)}, u32[]{:S(2)}, u32[]{:S(2)}) %all-to-all-start.1) | async-done | bytes 524320 | tf_op jit(solution)/shard_map/all_to_all | solution.py:40
  305.6 0.7 fusion.1
  306.3 1.0 copy.13
  307.3 75.8 %reduce-scatter.8.cloned.1.call-done = f32[128,128]{1,0:T(8,128)} async-done(((f32[128,1024]{1,0:T(8,128)}), f32[128,128]{1,0:T(8,128)}) %reduce-scatter.8.cloned.1.call-update) | async-done | bytes 65552 | tf_op jit(solution)/shard_map/reduce_scatter | solution.py:52
  383.1 1.5 convert_element_type.31
  (11 shorter events, 0.1 us)
Async XLA Ops:
  7.2 69.1 %all-gather.4.cloned.1.call-start = ((), (), s32[]{:S(2)}) async-start(), calls=%async_computation.5 | async-start | bytes 4718592 | tf_op jit(solution)/shard_map/all_gather | solution.py:9
  7.9 127.0 %all-gather.6.cloned.1.call-start = ((), (), s32[]{:S(2)}) async-start(), calls=%async_computation.7 | async-start | bytes 4718592 | tf_op jit(solution)/shard_map/all_gather | solution.py:10
  8.6 170.5 %reduce-scatter.4.cloned.1.call-start = ((), (), s32[]{:S(2)}) async-start(), calls=%async_computation.6 | async-start | bytes 1179648 | tf_op jit(solution)/shard_map/reduce_scatter | solution.py:23
  54.0 84.8 %copy-start.1 = (bf16[128,1024]{1,0:T(8,128)(2,1)}, bf16[128,1024]{1,0:T(8,128)(2,1)S(1)}, u32[]{:S(2)}) copy-start(bf16[128,1024]{1,0:T(8,128)(2,1)S(1)} %all_gather.18) | copy-start | bytes 786436
  80.2 141.9 %copy-start.2 = (bf16[128,256]{1,0:T(8,128)(2,1)S(1)}, bf16[128,256]{1,0:T(8,128)(2,1)}, u32[]{:S(2)}) copy-start(bf16[128,256]{1,0:T(8,128)(2,1)} %param.7) | copy-start | bytes 196612
  80.2 141.9 %reduce-scatter.6.cloned.1.call-start = ((), (), s32[]{:S(2)}) async-start(), calls=%async_computation.8 | async-start | bytes 1179648 | tf_op jit(solution)/shard_map/reduce_scatter | solution.py:24
  138.9 155.9 %all-gather.8.cloned.1.call-start = ((), (), s32[]{:S(2)}) async-start(), calls=%async_computation.10 | async-start | bytes 2359296 | tf_op jit(solution)/shard_map/all_gather | solution.py:18
  250.1 35.1 %all-to-all-start = ((bf16[128,8,256]{2,0,1:T(8,128)(2,1)}), bf16[128,8,256]{2,0,1:T(8,128)(2,1)S(1)}, u32[]{:S(2)}, u32[]{:S(2)}) async-start(bf16[128,8,256]{2,0,1:T(8,128)(2,1)} %bitcast.29), calls=%async_computation.3 | async-start | bytes 1048576 | tf_op jit(solution)/shard_map/all_to_all | solution.py:39
  285.2 20.3 %all-to-all-start.1 = ((bf16[128,8,256]{2,0,1:T(8,128)(2,1)}), bf16[128,8,256]{2,0,1:T(8,128)(2,1)S(1)}, u32[]{:S(2)}, u32[]{:S(2)}) async-start(bf16[128,8,256]{2,0,1:T(8,128)(2,1)} %bitcast.28), calls=%async_computation.4 | async-start | bytes 1048576 | tf_op jit(solution)/shard_map/all_to_all | solution.py:40
  290.2 92.8 %reduce-scatter.8.cloned.1.call-start = ((), (), s32[]{:S(2)}) async-start(), calls=%async_computation.9 | async-start | bytes 589824 | tf_op jit(solution)/shard_map/reduce_scatter | solution.py:52
  294.8 10.8 %copy-start = (bf16[1024,1024]{1,0:T(8,128)(2,1)S(1)}, bf16[1024,1024]{1,0:T(8,128)(2,1)}, u32[]{:S(2)}) copy-start(bf16[1024,1024]{1,0:T(8,128)(2,1)} %all-gather.8.cloned.1.call-done) | copy-start | bytes 6291460
Sparse Core Ops, SparseCore 0:
  10.0 66.2 all-gather.3
  78.3 56.6 all-gather.5
  137.7 41.4 reduce-scatter.3
  181.9 40.1 reduce-scatter.5
  224.6 45.1 all-gather.7
  295.2 87.8 reduce-scatter.7
where the time goes:
time: 392 us; the launch traced here: 391 us
  waiting for transfers between devices  243 us (62%)
  blocking collectives  96.3 us (25%)
  matrix products  20 us (5%)
  between operations  14.2 us (4%)
  starting transfers between devices  10.3 us (3%)
  local copies, waits for them, and re-layouts  4.71 us (1%)
    reduce_scatter x1, waiting for transfers between devices, body(): lax.psum_scatter(input_part, 'gy', scatter_dimension=1, tiled=True)  75.8 us
    all_gather x1, waiting for transfers between devices, fetch_blocks(): lax.all_gather(up_weight, 'gx', axis=1, tiled=True)  54.7 us
    all_gather x1, blocking collectives, body(): block_rows = lax.all_gather(tokens, 'gy', axis=1, tiled=True)  45.3 us
    reduce_scatter x1, waiting for transfers between devices, body(): lax.psum_scatter(up_part, 'gz', scatter_dimension=1, tiled=True)  42.9 us
    reduce_scatter x1, waiting for transfers between devices, body(): lax.psum_scatter(gate_part, 'gz', scatter_dimension=1, tiled=True)  39.7 us
    all_gather x1, blocking collectives, body(): lax.all_gather(gate_grad, 'gz', axis=1, tiled=True)  25.5 us
    all_gather x1, blocking collectives, body(): lax.all_gather(up_grad, 'gz', axis=1, tiled=True)  25.5 us
    all_gather x1, waiting for transfers between devices, fetch_blocks(): lax.all_gather(gate_weight, 'gx', axis=1, tiled=True)  22.2 us
  transfers between devices with their start and end apart: 8, of which 6 were waited for; matrix products, arithmetic and copies ran while one was open for 7% of the time, Pallas kernels for 0%

commit v1 on v0

v1 whole, which is shorter than its diff:
```python
import jax
import jax.numpy as jnp
from jax import lax
from jax.sharding import Mesh, PartitionSpec as P

PLANE = ("zl", "x", "zh")
F32 = jnp.float32
BF16 = jnp.bfloat16


def regroup():
    pairs = []
    for zl in range(4):
        for co in range(2):
            for c in range(2):
                for a in range(4):
                    work = (zl * 2 + co) * 8 + 4 * c + a
                    home = (a * 2 + co) * 8 + 2 * zl + (co ^ c)
                    pairs.append((work, home))
    return pairs


def swap_cores(value):
    return lax.ppermute(value, "co", [(0, 1), (1, 0)])


def spread(value, axes, count):
    return lax.all_to_all(jnp.tile(value, (count, 1)), axes, 0, 0, tiled=True)


def body(tokens, gate_weight, up_weight, hidden_grad):
    to_home = regroup()
    to_work = [(home, work) for work, home in to_home]
    tiles = spread(tokens, PLANE, 32)
    own_weight = jnp.concatenate([gate_weight, up_weight], axis=1)
    other_weight = swap_cores(own_weight)
    upstream = lax.ppermute(hidden_grad, ("zl", "co", "y"), to_work)
    rows = tiles.reshape(4, 8, 128, 128).transpose(0, 2, 1, 3).reshape(512, 1024)
    own_part = jnp.dot(rows, own_weight, preferred_element_type=F32).astype(BF16)
    other_part = jnp.dot(rows, other_weight, preferred_element_type=F32).astype(BF16)
    parts = jnp.concatenate([own_part, other_part], axis=0)
    parts = lax.all_to_all(parts, "y", 0, 0, tiled=True)
    other_rows = swap_cores(rows)
    sums = jnp.sum(parts.reshape(8, 128, 512).astype(F32), axis=0)
    gate_sum, up_sum = sums[:, :256], sums[:, 256:]
    sigmoid_gate = jax.nn.sigmoid(gate_sum)
    activated = gate_sum * sigmoid_gate
    hidden = (activated * up_sum).astype(BF16)
    upstream = upstream.astype(F32)
    gate_grad = upstream * up_sum * sigmoid_gate * (1.0 + gate_sum * (1.0 - sigmoid_gate))
    up_grad = upstream * activated
    grads = jnp.concatenate([gate_grad.astype(BF16), up_grad.astype(BF16)], axis=1)
    grads = spread(grads, "y", 8)
    own_grads, other_grads = grads[:512], grads[512:]
    contract_last = (((1,), (1,)), ((), ()))
    input_part = lax.dot_general(own_grads, own_weight, contract_last, preferred_element_type=F32)
    input_part += lax.dot_general(
        other_grads, other_weight, contract_last, preferred_element_type=F32
    )
    blocks = input_part.astype(BF16).reshape(4, 128, 8, 128).transpose(0, 2, 1, 3)
    blocks = lax.all_to_all(blocks.reshape(32 * 128, 128), PLANE, 0, 0, tiled=True)
    hidden = lax.ppermute(hidden, ("zl", "co", "y"), to_home)
    received_grads = swap_cores(other_grads)
    contract_rows = (((0,), (0,)), ((), ()))
    wgrad = lax.dot_general(rows, own_grads, contract_rows, preferred_element_type=F32)
    wgrad += lax.dot_general(other_rows, received_grads, contract_rows, preferred_element_type=F32)
    wgrad = wgrad.astype(BF16)
    input_grad = jnp.sum(blocks.reshape(32, 128, 128).astype(F32), axis=0).astype(BF16)
    return hidden, input_grad, wgrad[:, :256], wgrad[:, 256:]


def solution(mesh):
    fine = Mesh(mesh.devices.reshape(4, 2, 4, 2, 8), ("zl", "co", "x", "zh", "y"))
    gx, gy, gz = ("zl", "co"), ("x", "zh"), ("y",)
    in_specs = (P(gx, gz + gy), P(gz, gy + gx), P(gz, gy + gx), P(gx, gy + gz))
    out_specs = (P(gx, gy + gz), P(gx, gz + gy), P(gz, gy + gx), P(gz, gy + gx))
    return jax.shard_map(body, mesh=fine, in_specs=in_specs, out_specs=out_specs, check_vma=False)
```

time: 392 us -> 162 us (0.41)
  waiting for transfers between devices: 243 us -> 73.8 us
  blocking collectives: 96.3 us -> 33.3 us
  starting transfers between devices: 10.3 us -> 37.3 us
  between operations: 14.2 us -> 0.89 us
  matrix products: 20 us -> 6.81 us
    reduce_scatter x3 -> x0, waiting for transfers between devices: 158 us -> none  [the longest x1 75.8 us: body(): lax.psum_scatter(input_part, 'gy', scatter_dimension=1, tiled=True)]
    all_gather x3 -> x0, blocking collectives: 96.3 us -> none  [the longest x1 45.3 us: body(): block_rows = lax.all_gather(tokens, 'gy', axis=1, tiled=True)]
    all_gather x3 -> x0, waiting for transfers between devices: 76.9 us -> none  [the longest x1 54.7 us: fetch_blocks(): lax.all_gather(up_weight, 'gx', axis=1, tiled=True)]
    all_to_all x2 -> x3, waiting for transfers between devices: 5.45 us -> 73.7 us  [the longest x1 25.7 us: spread(): return lax.all_to_all(jnp.tile(value, (count, 1)), axes, 0, 0, tiled=True)]
    all_to_all x0 -> x1, blocking collectives: none -> 33.3 us  [spread(): return lax.all_to_all(jnp.tile(value, (count, 1)), axes, 0, 0, tiled=True)]
    all_to_all x2 -> x3, starting transfers between devices: 10.1 us -> 29.7 us  [the longest x1 13.4 us: spread(): return lax.all_to_all(jnp.tile(value, (count, 1)), axes, 0, 0, tiled=True)]
    dot_general x6, matrix products: 20 us -> 6.81 us  [the longest x1 1.98 us: body(): lax.dot_general(other_grads, other_weight, contract_last, preferred_eleme...]
    ppermute x0 -> x5, starting transfers between devices: none -> 7.58 us  [the longest x3 6.25 us: swap_cores(): return lax.ppermute(value, 'co', [(0, 1), (1, 0)])]
  transfers between devices with their start and end apart: 8 -> 8, of which waited for: 6 -> 4; matrix products, arithmetic and copies ran while one was open for 7% -> 3% of each run, Pallas kernels for 0% -> 0%
where the time goes in v1:
time: 162 us
  waiting for transfers between devices  73.8 us (46%)
  starting transfers between devices  37.3 us (23%)
  blocking collectives  33.3 us (21%)
  local copies, waits for them, and re-layouts  7.45 us (5%)
  matrix products  6.81 us (4%)
  other arithmetic  2.09 us (1%)
    all_to_all x1, blocking collectives, spread(): return lax.all_to_all(jnp.tile(value, (count, 1)), axes, 0, 0, tiled=True)  33.3 us
    all_to_all x1, waiting for transfers between devices, spread(): return lax.all_to_all(jnp.tile(value, (count, 1)), axes, 0, 0, tiled=True)  25.7 us
    all_to_all x1, waiting for transfers between devices, body(): lax.all_to_all(blocks.reshape(32 * 128, 128), PLANE, 0, 0, tiled=True)  24.1 us
    all_to_all x1, waiting for transfers between devices, body(): parts = lax.all_to_all(parts, 'y', 0, 0, tiled=True)  23.8 us
    all_to_all x1, starting transfers between devices, spread(): return lax.all_to_all(jnp.tile(value, (count, 1)), axes, 0, 0, tiled=True)  13.4 us
    all_to_all x1, starting transfers between devices, body(): lax.all_to_all(blocks.reshape(32 * 128, 128), PLANE, 0, 0, tiled=True)  9.21 us
    all_to_all x1, starting transfers between devices, body(): parts = lax.all_to_all(parts, 'y', 0, 0, tiled=True)  7.1 us
    ppermute x3, starting transfers between devices, swap_cores(): return lax.ppermute(value, 'co', [(0, 1), (1, 0)])  6.25 us
  transfers between devices with their start and end apart: 8, of which 4 were waited for; matrix products, arithmetic and copies ran while one was open for 3% of the time, Pallas kernels for 0%

profile of v1, /device:TPU:6, one launch (start us, length us, event | category | flops | bytes accessed | tf_op | source)
XLA Modules:
  0.0 161.6 jit_solution(1111892721425423101)
XLA Ops:
  0.7 2.1 %tile.4 = bf16[32,128,128]{2,1,0:T(8,128)(2,1)} broadcast(bf16[128,128]{1,0:T(8,128)(2,1)} %param.4), dimensions={1,2} | broadcast | bytes 1081344 | tf_op jit(solution)/shard_map/tile | solution.py:28
  2.7 13.4 %all-to-all-start = ((bf16[32,128,128]{2,1,0:T(8,128)(2,1)}), bf16[32,128,128]{2,1,0:T(8,128)(2,1)S(1)}, u32[]{:S(2)}, u32[]{:S(2)}) async-start(bf16[32,128,128]{2,1,0:T(8,128)(2,1)} %tile.4), calls=%async_computation | async-start | bytes 2097152 | tf_op jit(solution)/shard_map/all_to_all | solution.py:28
  16.3 1.9 %collective-permute-start = (bf16[1024,512]{1,0:T(8,128)(2,1)S(1)}, bf16[1024,512]{1,0:T(8,128)(2,1)}, u32[]{:S(2)}, u32[]{:S(2)}) collective-permute-start(bf16[1024,512]{1,0:T(8,128)(2,1)S(1)} %constant_dynamic-update-slice_fusion), channel_id=1, source_target_pairs={{0,64},{64,0},{1,65},{65,1},{2,66},{66,2},{3,67},{67,3},{4,68},{68... | collective-permute-start | bytes 3145736 | tf_op jit(solution)/shard_map/ppermute | solution.py:24
  18.2 25.7 %all-to-all-done = bf16[32,128,128]{2,1,0:T(8,128)(2,1)S(1)} async-done(((bf16[32,128,128]{2,1,0:T(8,128)(2,1)}), bf16[32,128,128]{2,1,0:T(8,128)(2,1)S(1)}, u32[]{:S(2)}, u32[]{:S(2)}) %all-to-all-start) | async-done | bytes 1048608 | tf_op jit(solution)/shard_map/all_to_all | solution.py:28
  43.9 0.7 copy.13
  44.6 0.7 fusion.2
  45.3 1.9 %fusion.3 = bf16[512,512]{1,0:T(8,128)(2,1)S(1)} fusion(bf16[1024,512]{1,0:T(8,128)(2,1)} %collective-permute-done, bf16[64,8,8,128]{3,2,1,0:T(8,128)(2,1)S(1)} %bitcast.37), kind=kOutput, calls=%fused_computation.8 | convolution fusion | flops 537133056 | bytes 2621440 | tf_op jit(solution)/shard_map/dot_general | solution.py:40
  47.2 1.1 pad_maximum_fusion
  48.3 7.1 %all-to-all-start.1 = ((bf16[8,128,512]{2,1,0:T(8,128)(2,1)}), bf16[8,128,512]{2,1,0:T(8,128)(2,1)S(1)}, u32[]{:S(2)}, u32[]{:S(2)}) async-start(bf16[8,128,512]{2,1,0:T(8,128)(2,1)} %bitcast.4), calls=%async_computation.1 | async-start | bytes 2097152 | tf_op jit(solution)/shard_map/all_to_all | solution.py:42
  55.4 0.7 collective-permute-start.2
  56.1 23.8 %all-to-all-done.1 = bf16[8,128,512]{2,1,0:T(8,128)(2,1)S(1)} async-done(((bf16[8,128,512]{2,1,0:T(8,128)(2,1)}), bf16[8,128,512]{2,1,0:T(8,128)(2,1)S(1)}, u32[]{:S(2)}, u32[]{:S(2)}) %all-to-all-start.1) | async-done | bytes 1048608 | tf_op jit(solution)/shard_map/all_to_all | solution.py:42
  79.9 0.1 convert_reduce_fusion
  80.1 0.1 fusion.6
  80.2 0.1 tile.5
  80.3 33.3 %all_to_all.30 = bf16[8,128,512]{2,1,0:T(8,128)(2,1)S(1)} all-to-all(bf16[8,128,512]{2,1,0:T(8,128)(2,1)S(1)} %tile.5), channel_id=1, replica_groups=mesh['zl'=4,'co'=2,'x'=4,'zh'=2,'y'=8] {'y'}, dimensions={0} | all-to-all | bytes 2097152 | tf_op jit(solution)/shard_map/all_to_all | solution.py:28
  113.6 0.7 fusion.12
  114.4 2.0 %fusion = bf16[64,8,8,128]{3,1,2,0:T(8,128)(2,1)S(1)} fusion(f32[512,1024]{1,0:T(8,128)S(1)} %fusion.12, bf16[512,512]{1,0:T(8,128)(2,1)S(1)} %bitcast.45, bf16[1024,512]{1,0:T(8,128)(2,1)} %collective-permute-done), kind=kOutput, calls=%fused_computation.3 | convolution fusion | flops 537919488 | bytes 4718592 | tf_op jit(solution)/shard_map/dot_general | solution.py:57
  116.4 0.3 copy.18
  116.7 1.2 copy.14
  117.9 9.2 %all-to-all-start.3 = ((bf16[32,128,128]{2,1,0:T(8,128)(2,1)}), bf16[32,128,128]{2,1,0:T(8,128)(2,1)S(1)}, u32[]{:S(2)}, u32[]{:S(2)}) async-start(bf16[32,128,128]{2,1,0:T(8,128)(2,1)} %bitcast.42), calls=%async_computation.3 | async-start | bytes 2097152 | tf_op jit(solution)/shard_map/all_to_all | solution.py:61
  127.1 0.3 copy.23
  127.4 1.9 %collective-permute-start.4 = (bf16[512,1024]{1,0:T(8,128)(2,1)S(1)}, bf16[512,1024]{1,0:T(8,128)(2,1)S(1)}, u32[]{:S(2)}, u32[]{:S(2)}) collective-permute-start(bf16[512,1024]{1,0:T(8,128)(2,1)S(1)} %bitcast.47), channel_id=1, source_target_pairs={{0,64},{64,0},{1,65},{65,1},{2,66},{66,2},{3,67},{67,3},{4,68},{68... | collective-permute-start | bytes 3145736 | tf_op jit(solution)/shard_map/ppermute | solution.py:24
  129.3 2.4 %collective-permute-start.3 = (bf16[512,512]{1,0:T(8,128)(2,1)S(1)}, bf16[512,512]{1,0:T(8,128)(2,1)S(1)}, u32[]{:S(2)}, u32[]{:S(2)}) collective-permute-start(bf16[512,512]{1,0:T(8,128)(2,1)S(1)} %bitcast.46), channel_id=1, source_target_pairs={{0,64},{64,0},{1,65},{65,1},{2,66},{66,2},{3,67},{67,3},{4,68},{68... | collective-permute-start | bytes 1572872 | tf_op jit(solution)/shard_map/ppermute | solution.py:24
  131.7 0.7 collective-permute-start.1
  132.4 0.7 fusion.9
  133.2 0.1 collective-permute-done.3
  133.2 0.7 fusion.1
  134.1 1.0 copy.15
  135.1 1.0 copy.16
  136.1 24.1 %all-to-all-done.3 = bf16[32,128,128]{2,1,0:T(8,128)(2,1)S(1)} async-done(((bf16[32,128,128]{2,1,0:T(8,128)(2,1)}), bf16[32,128,128]{2,1,0:T(8,128)(2,1)S(1)}, u32[]{:S(2)}, u32[]{:S(2)}) %all-to-all-start.3) | async-done | bytes 1048608 | tf_op jit(solution)/shard_map/all_to_all | solution.py:61
  160.2 0.8 reduce_sum.22
  160.9 0.6 copy.26
  (19 shorter events, 0.3 us)
Async XLA Ops:
  0.6 15.5 %copy-start.2 = (bf16[1024,256]{1,0:T(8,128)(2,1)S(1)}, bf16[1024,256]{1,0:T(8,128)(2,1)}, u32[]{:S(2)}) copy-start(bf16[1024,256]{1,0:T(8,128)(2,1)} %param.5) | copy-start | bytes 1572868
  0.6 15.6 %copy-start.3 = (bf16[1024,256]{1,0:T(8,128)(2,1)S(1)}, bf16[1024,256]{1,0:T(8,128)(2,1)}, u32[]{:S(2)}) copy-start(bf16[1024,256]{1,0:T(8,128)(2,1)} %param.6) | copy-start | bytes 1572868
  2.7 41.1 %all-to-all-start = ((bf16[32,128,128]{2,1,0:T(8,128)(2,1)}), bf16[32,128,128]{2,1,0:T(8,128)(2,1)S(1)}, u32[]{:S(2)}, u32[]{:S(2)}) async-start(bf16[32,128,128]{2,1,0:T(8,128)(2,1)} %tile.4), calls=%async_computation | async-start | bytes 2097152 | tf_op jit(solution)/shard_map/all_to_all | solution.py:28
  16.3 29.0 %collective-permute-start = (bf16[1024,512]{1,0:T(8,128)(2,1)S(1)}, bf16[1024,512]{1,0:T(8,128)(2,1)}, u32[]{:S(2)}, u32[]{:S(2)}) collective-permute-start(bf16[1024,512]{1,0:T(8,128)(2,1)S(1)} %constant_dynamic-update-slice_fusion), channel_id=1, source_target_pairs={{0,64},{64,0},{1,65},{65,1},{2,66},{66,2},{3,67},{67,3},{4,68},{68... | collective-permute-start | bytes 3145736 | tf_op jit(solution)/shard_map/ppermute | solution.py:24
  47.2 8.2 %copy-start.4 = (bf16[128,256]{1,0:T(8,128)(2,1)S(1)}, bf16[128,256]{1,0:T(8,128)(2,1)}, u32[]{:S(2)}) copy-start(bf16[128,256]{1,0:T(8,128)(2,1)} %param.7) | copy-start | bytes 196612
  48.3 31.6 %all-to-all-start.1 = ((bf16[8,128,512]{2,1,0:T(8,128)(2,1)}), bf16[8,128,512]{2,1,0:T(8,128)(2,1)S(1)}, u32[]{:S(2)}, u32[]{:S(2)}) async-start(bf16[8,128,512]{2,1,0:T(8,128)(2,1)} %bitcast.4), calls=%async_computation.1 | async-start | bytes 2097152 | tf_op jit(solution)/shard_map/all_to_all | solution.py:42
  55.4 24.7 %collective-permute-start.2 = (bf16[128,256]{1,0:T(8,128)(2,1)S(1)}, bf16[128,256]{1,0:T(8,128)(2,1)S(1)}, u32[]{:S(2)}, u32[]{:S(2)}) collective-permute-start(bf16[128,256]{1,0:T(8,128)(2,1)S(1)} %copy-done.4), channel_id=1, source_target_pairs={{0,0},{128,1},{256,2},{384,3},{1,4},{129,5},{257,6},{385,7},{65,64... | collective-permute-start | bytes 196616 | tf_op jit(solution)/shard_map/ppermute | solution.py:37
  113.6 2.7 %copy-start = (bf16[4,128,512]{2,1,0:T(8,128)(2,1)}, bf16[4,128,512]{2,1,0:T(8,128)(2,1)S(1)}, u32[]{:S(2)}) copy-start(bf16[4,128,512]{2,1,0:T(8,128)(2,1)S(1)} %get-tuple-element.18) | copy-start | bytes 1572868
  117.9 11.4 %copy-start.1 = (bf16[4,128,512]{2,1,0:T(8,128)(2,1)S(1)}, bf16[4,128,512]{2,1,0:T(8,128)(2,1)}, u32[]{:S(2)}) copy-start(bf16[4,128,512]{2,1,0:T(8,128)(2,1)} %copy-done) | copy-start | bytes 1572868
  117.9 42.3 %all-to-all-start.3 = ((bf16[32,128,128]{2,1,0:T(8,128)(2,1)}), bf16[32,128,128]{2,1,0:T(8,128)(2,1)S(1)}, u32[]{:S(2)}, u32[]{:S(2)}) async-start(bf16[32,128,128]{2,1,0:T(8,128)(2,1)} %bitcast.42), calls=%async_computation.3 | async-start | bytes 2097152 | tf_op jit(solution)/shard_map/all_to_all | solution.py:61
  127.4 5.8 %collective-permute-start.4 = (bf16[512,1024]{1,0:T(8,128)(2,1)S(1)}, bf16[512,1024]{1,0:T(8,128)(2,1)S(1)}, u32[]{:S(2)}, u32[]{:S(2)}) collective-permute-start(bf16[512,1024]{1,0:T(8,128)(2,1)S(1)} %bitcast.47), channel_id=1, source_target_pairs={{0,64},{64,0},{1,65},{65,1},{2,66},{66,2},{3,67},{67,3},{4,68},{68... | collective-permute-start | bytes 3145736 | tf_op jit(solution)/shard_map/ppermute | solution.py:24
  129.3 3.9 %collective-permute-start.3 = (bf16[512,512]{1,0:T(8,128)(2,1)S(1)}, bf16[512,512]{1,0:T(8,128)(2,1)S(1)}, u32[]{:S(2)}, u32[]{:S(2)}) collective-permute-start(bf16[512,512]{1,0:T(8,128)(2,1)S(1)} %bitcast.46), channel_id=1, source_target_pairs={{0,64},{64,0},{1,65},{65,1},{2,66},{66,2},{3,67},{67,3},{4,68},{68... | collective-permute-start | bytes 1572872 | tf_op jit(solution)/shard_map/ppermute | solution.py:24
  131.7 0.7 collective-permute-start.1

commit v2 on v1

v2 whole, which is shorter than its diff:
```python
import jax
import jax.numpy as jnp
from jax import lax
from jax.sharding import Mesh, PartitionSpec as P

PLANE = ("x", "zl", "zh")
F32 = jnp.float32
BF16 = jnp.bfloat16
LAST = (((1,), (1,)), ((), ()))
ROWS = (((0,), (0,)), ((), ()))


def regroup():
    pairs = []
    for zl in range(4):
        for co in range(2):
            for q in range(4):
                for p in range(2):
                    work = (zl * 2 + co) * 8 + 2 * q + p
                    home = (q * 2 + co) * 8 + 2 * zl + p
                    pairs.append((work, home))
    return pairs


def swap_cores(value):
    return lax.ppermute(value, "co", [(0, 1), (1, 0)])


def swap_pair(value):
    return lax.ppermute(value, "yp", [(0, 1), (1, 0)])


def body(tokens, gate_weight, up_weight, hidden_grad):
    core, side = lax.axis_index("co"), lax.axis_index("yp")
    low, own_first = side == 0, side == core
    perm = regroup()
    everyone = ("zl", "co", "yq", "yp")

    def split(value):
        return jnp.where(low, value[:64], value[64:]), jnp.where(low, value[64:], value[:64])

    def join(kept, received):
        return jnp.where(
            low, jnp.concatenate([kept, received]), jnp.concatenate([received, kept])
        )

    kept, sent = split(tokens)
    pair_tokens = jnp.concatenate([kept, swap_pair(sent)], axis=1)
    tiles = lax.all_to_all(jnp.tile(pair_tokens, (32, 1)), PLANE, 0, 0, tiled=True)
    own = jnp.concatenate([gate_weight, up_weight], axis=1)
    own_pair = swap_pair(own)
    other = swap_cores(own)
    other_pair = swap_cores(own_pair)
    upstream = lax.ppermute(hidden_grad, everyone, [(home, work) for work, home in perm])
    kept, sent = split(upstream)
    received = swap_pair(sent)
    upstream = jnp.where(
        own_first,
        jnp.concatenate([kept, received], axis=1),
        jnp.concatenate([received, kept], axis=1),
    ).astype(F32)

    rows = tiles.reshape(4, 4, 2, 64, 2, 128).transpose(1, 3, 4, 0, 2, 5).reshape(256, 2048)
    near_rows, far_rows = rows[:, :1024], rows[:, 1024:]

    def forward(near, far):
        return (
            jnp.dot(near_rows, near, preferred_element_type=F32)
            + jnp.dot(far_rows, far, preferred_element_type=F32)
        ).astype(BF16)

    parts = jnp.concatenate([forward(own, own_pair), forward(other, other_pair)], axis=1)
    parts = lax.all_to_all(parts, "yq", 0, 0, tiled=True)
    sums = jnp.sum(parts.reshape(4, 64, 1024).astype(F32), axis=0)
    gate_sum = jnp.concatenate([sums[:, :256], sums[:, 512:768]], axis=1)
    up_sum = jnp.concatenate([sums[:, 256:512], sums[:, 768:]], axis=1)
    sigmoid_gate = jax.nn.sigmoid(gate_sum)
    activated = gate_sum * sigmoid_gate
    hidden = (activated * up_sum).astype(BF16)
    gate_grad = upstream * up_sum * sigmoid_gate * (1.0 + gate_sum * (1.0 - sigmoid_gate))
    up_grad = upstream * activated
    gate_grad, up_grad = gate_grad.astype(BF16), up_grad.astype(BF16)
    grads = jnp.concatenate(
        [gate_grad[:, :256], up_grad[:, :256], gate_grad[:, 256:], up_grad[:, 256:]], axis=1
    )
    grads = lax.all_to_all(jnp.tile(grads, (4, 1)), "yq", 0, 0, tiled=True)
    own_grads, other_grads = grads[:, :512], grads[:, 512:]

    def backward(mine, others):
        return (
            lax.dot_general(own_grads, mine, LAST, preferred_element_type=F32)
            + lax.dot_general(other_grads, others, LAST, preferred_element_type=F32)
        ).astype(BF16)

    block = jnp.stack([backward(own, other), backward(own_pair, other_pair)])
    block = block.reshape(2, 4, 64, 4, 2, 128).transpose(3, 1, 4, 2, 0, 5).reshape(32 * 64, 256)
    block = lax.all_to_all(block, PLANE, 0, 0, tiled=True)

    kept = jnp.where(own_first, hidden[:, :256], hidden[:, 256:])
    sent = jnp.where(own_first, hidden[:, 256:], hidden[:, :256])
    hidden = lax.ppermute(join(kept, swap_pair(sent)), everyone, perm)

    pair_rows, pair_grads = swap_pair(far_rows), swap_pair(grads)
    mine_rows = jnp.concatenate([near_rows, pair_rows])
    mine_grads = jnp.concatenate([own_grads, pair_grads[:, :512]])
    their_grads = jnp.concatenate([other_grads, pair_grads[:, 512:]])
    wgrad = lax.dot_general(mine_rows, mine_grads, ROWS, preferred_element_type=F32)
    wgrad += lax.dot_general(
        swap_cores(mine_rows), swap_cores(their_grads), ROWS, preferred_element_type=F32
    )
    wgrad = wgrad.astype(BF16)
    block = jnp.sum(block.reshape(32, 64, 256).astype(F32), axis=0).astype(BF16)
    input_grad = join(block[:, :128], swap_pair(block[:, 128:]))
    return hidden, input_grad, wgrad[:, :256], wgrad[:, 256:]


def solution(mesh):
    axes = ("zl", "co", "x", "zh", "yq", "yp")
    fine = Mesh(mesh.devices.reshape(4, 2, 4, 2, 4, 2), axes)
    gx, gy, gz = ("zl", "co"), ("x", "zh"), ("yq", "yp")
    in_specs = (P(gx, gz + gy), P(gz, gy + gx), P(gz, gy + gx), P(gx, gy + gz))
    out_specs = (P(gx, gy + gz), P(gx, gz + gy), P(gz, gy + gx), P(gz, gy + gx))
    return jax.shard_map(body, mesh=fine, in_specs=in_specs, out_specs=out_specs, check_vma=False)
```

time: 162 us -> 177 us (1.093)
  the two profiles are of different devices: /device:TPU:6 before, /device:TPU:128 now
where the time goes in v2:
time: 177 us; the launch traced here: 175 us
  starting transfers between devices  71.1 us (40%)
  waiting for transfers between devices  65.3 us (37%)
  local copies, waits for them, and re-layouts  17.2 us (10%)
  matrix products  14.6 us (8%)
  other arithmetic  6.24 us (4%)
    ppermute x7, waiting for transfers between devices, swap_pair(): return lax.ppermute(value, 'yp', [(0, 1), (1, 0)])  29.9 us
    ppermute x7, starting transfers between devices, swap_pair(): return lax.ppermute(value, 'yp', [(0, 1), (1, 0)])  21.7 us
    all_to_all x1, waiting for transfers between devices, body(): grads = lax.all_to_all(jnp.tile(grads, (4, 1)), 'yq', 0, 0, tiled=True)  13.7 us
    ppermute x1, waiting for transfers between devices, body(): lax.ppermute(hidden_grad, everyone, [(home, work) for work, home in perm])  11.7 us
    all_to_all x1, starting transfers between devices, body(): lax.all_to_all(jnp.tile(pair_tokens, (32, 1)), PLANE, 0, 0, tiled=True)  11.7 us
    ppermute x1, waiting for transfers between devices, body(): hidden = lax.ppermute(join(kept, swap_pair(sent)), everyone, perm)  9.93 us
    ppermute x4, starting transfers between devices, swap_cores(): return lax.ppermute(value, 'co', [(0, 1), (1, 0)])  8.16 us
    all_to_all x1, starting transfers between devices, body(): block = lax.all_to_all(block, PLANE, 0, 0, tiled=True)  8.06 us
  transfers between devices with their start and end apart: 17, of which 8 were waited for; matrix products, arithmetic and copies ran while one was open for 17% of the time, Pallas kernels for 0%

profile of v2, /device:TPU:128, one launch (start us, length us, event | category | flops | bytes accessed | tf_op | source)
XLA Modules:
  0.0 175.5 jit_solution(12599083487996019397)
XLA Ops:
  1.4 3.5 %collective-permute-start = (bf16[64,128]{1,0:T(8,128)(2,1)S(1)}, bf16[64,128]{1,0:T(8,128)(2,1)S(1)}, u32[]{:S(2)}, u32[]{:S(2)}) collective-permute-start(bf16[64,128]{1,0:T(8,128)(2,1)S(1)} %get-tuple-element.30), channel_id=1, source_target_pairs={{0,1},{1,0},{2,3},{3,2},{4,5},{5,4},{6,7},{7,6},{8,9},{9,8},{10,11... | collective-permute-start | bytes 49160 | tf_op jit(solution)/shard_map/ppermute | solution.py:30
  4.9 2.1 %collective-permute-done = bf16[64,128]{1,0:T(8,128)(2,1)S(1)} collective-permute-done((bf16[64,128]{1,0:T(8,128)(2,1)S(1)}, bf16[64,128]{1,0:T(8,128)(2,1)S(1)}, u32[]{:S(2)}, u32[]{:S(2)}) %collective-permute-start) | collective-permute-done | bytes 16416 | tf_op jit(solution)/shard_map/ppermute | solution.py:30
  8.2 11.7 %all-to-all-start = ((bf16[32,64,256]{2,1,0:T(8,128)(2,1)}), bf16[32,64,256]{2,1,0:T(8,128)(2,1)S(1)}, u32[]{:S(2)}, u32[]{:S(2)}) async-start(bf16[32,64,256]{2,1,0:T(8,128)(2,1)} %tile.4), calls=%async_computation | async-start | bytes 2097152 | tf_op jit(solution)/shard_map/all_to_all | solution.py:49
  19.9 3.5 %collective-permute-start.1 = (bf16[1024,512]{1,0:T(8,128)(2,1)S(1)}, bf16[1024,512]{1,0:T(8,128)(2,1)}, u32[]{:S(2)}, u32[]{:S(2)}) collective-permute-start(bf16[1024,512]{1,0:T(8,128)(2,1)S(1)} %constant_dynamic-update-slice_fusion), channel_id=1, source_target_pairs={{0,1},{1,0},{2,3},{3,2},{4,5},{5,4},{6,7},{7,6},{8,9},{9,8},{10,11... | collective-permute-start | bytes 3145736 | tf_op jit(solution)/shard_map/ppermute | solution.py:30
  23.4 1.9 %collective-permute-start.2 = (bf16[1024,512]{1,0:T(8,128)(2,1)S(1)}, bf16[1024,512]{1,0:T(8,128)(2,1)}, u32[]{:S(2)}, u32[]{:S(2)}) collective-permute-start(bf16[1024,512]{1,0:T(8,128)(2,1)S(1)} %constant_dynamic-update-slice_fusion), channel_id=1, source_target_pairs={{0,64},{64,0},{1,65},{65,1},{2,66},{66,2},{3,67},{67,3},{4,68},{68... | collective-permute-start | bytes 3145736 | tf_op jit(solution)/shard_map/ppermute | solution.py:26
  25.4 19.8 %collective-permute-done.1 = bf16[1024,512]{1,0:T(8,128)(2,1)} collective-permute-done((bf16[1024,512]{1,0:T(8,128)(2,1)S(1)}, bf16[1024,512]{1,0:T(8,128)(2,1)}, u32[]{:S(2)}, u32[]{:S(2)}) %collective-permute-start.1) | collective-permute-done | bytes 1048608 | tf_op jit(solution)/shard_map/ppermute | solution.py:30
  45.1 1.9 %collective-permute-start.3 = (bf16[1024,512]{1,0:T(8,128)(2,1)}, bf16[1024,512]{1,0:T(8,128)(2,1)}, u32[]{:S(2)}, u32[]{:S(2)}) collective-permute-start(bf16[1024,512]{1,0:T(8,128)(2,1)} %collective-permute-done.1), channel_id=1, source_target_pairs={{0,64},{64,0},{1,65},{65,1},{2,66},{66,2},{3,67},{67,3},{4,68},{68... | collective-permute-start | bytes 3145736 | tf_op jit(solution)/shard_map/ppermute | solution.py:26
  48.2 3.9 %copy.10 = bf16[4,64,2,4,2,128]{5,4,3,2,1,0:T(2,128)(2,1)} copy(bf16[4,64,2,4,2,128]{5,2,1,4,0,3:T(2,128)(2,1)} %bitcast.21) | data formatting | bytes 2097152 | tf_op jit(solution)/shard_map/transpose | solution.py:63
  52.0 1.8 %reshape.45 = bf16[256,2048]{1,0:T(8,128)(2,1)S(1)} reshape(bf16[4,64,2,4,2,128]{5,4,3,2,1,0:T(2,128)(2,1)} %copy.10) | data formatting | bytes 2097152 | tf_op jit(solution)/shard_map/reshape | solution.py:63
  57.7 1.7 fusion.3
  60.2 7.1 %all-to-all-start.1 = ((bf16[4,64,1024]{2,1,0:T(8,128)(2,1)}), bf16[4,64,1024]{2,1,0:T(8,128)(2,1)S(1)}, u32[]{:S(2)}, u32[]{:S(2)}) async-start(bf16[4,64,1024]{2,1,0:T(8,128)(2,1)} %bitcast.1), calls=%async_computation.1 | async-start | bytes 1048576 | tf_op jit(solution)/shard_map/all_to_all | solution.py:73
  67.3 7.8 %collective-permute-start.6 = (bf16[128,256]{1,0:T(8,128)(2,1)S(1)}, bf16[128,256]{1,0:T(8,128)(2,1)S(1)}, u32[]{:S(2)}, u32[]{:S(2)}) collective-permute-start(bf16[128,256]{1,0:T(8,128)(2,1)S(1)} %copy-done.4), channel_id=1, source_target_pairs={{0,0},{1,1},{128,2},{129,3},{256,4},{257,5},{384,6},{385,7},{64,64... | collective-permute-start | bytes 196616 | tf_op jit(solution)/shard_map/ppermute | solution.py:54
  75.1 11.7 %collective-permute-done.6 = bf16[128,256]{1,0:T(8,128)(2,1)S(1)} collective-permute-done((bf16[128,256]{1,0:T(8,128)(2,1)S(1)}, bf16[128,256]{1,0:T(8,128)(2,1)S(1)}, u32[]{:S(2)}, u32[]{:S(2)}) %collective-permute-start.6) | collective-permute-done | bytes 65568 | tf_op jit(solution)/shard_map/ppermute | solution.py:54
  86.8 2.5 %collective-permute-start.7 = (bf16[64,256]{1,0:T(8,128)(2,1)S(1)}, bf16[64,256]{1,0:T(8,128)(2,1)S(1)}, u32[]{:S(2)}, u32[]{:S(2)}) collective-permute-start(bf16[64,256]{1,0:T(8,128)(2,1)S(1)} %get-tuple-element.23), channel_id=1, source_target_pairs={{0,1},{1,0},{2,3},{3,2},{4,5},{5,4},{6,7},{7,6},{8,9},{9,8},{10,11... | collective-permute-start | bytes 98312 | tf_op jit(solution)/shard_map/ppermute | solution.py:30
  89.5 3.2 %collective-permute-done.7 = bf16[64,256]{1,0:T(8,128)(2,1)S(1)} collective-permute-done((bf16[64,256]{1,0:T(8,128)(2,1)S(1)}, bf16[64,256]{1,0:T(8,128)(2,1)S(1)}, u32[]{:S(2)}, u32[]{:S(2)}) %collective-permute-start.7) | collective-permute-done | bytes 32800 | tf_op jit(solution)/shard_map/ppermute | solution.py:30
  93.6 4.7 %all-to-all-start.2 = ((bf16[4,64,1024]{2,1,0:T(8,128)(2,1)}), bf16[4,64,1024]{2,1,0:T(8,128)(2,1)S(1)}, u32[]{:S(2)}, u32[]{:S(2)}) async-start(bf16[4,64,1024]{2,1,0:T(8,128)(2,1)} %tile.5), calls=%async_computation.2 | async-start | bytes 1048576 | tf_op jit(solution)/shard_map/all_to_all | solution.py:86
  99.4 3.5 %collective-permute-start.9 = (bf16[256,1024]{1,0:T(8,128)(2,1)}, bf16[256,1024]{1,0:T(8,128)(2,1)}, u32[]{:S(2)}, u32[]{:S(2)}) collective-permute-start(bf16[256,1024]{1,0:T(8,128)(2,1)} %get-tuple-element.7), channel_id=1, source_target_pairs={{0,1},{1,0},{2,3},{3,2},{4,5},{5,4},{6,7},{7,6},{8,9},{9,8},{10,11... | collective-permute-start | bytes 1572872 | tf_op jit(solution)/shard_map/ppermute | solution.py:30
  102.9 13.7 %all-to-all-done.2 = bf16[4,64,1024]{2,1,0:T(8,128)(2,1)S(1)} async-done(((bf16[4,64,1024]{2,1,0:T(8,128)(2,1)}), bf16[4,64,1024]{2,1,0:T(8,128)(2,1)S(1)}, u32[]{:S(2)}, u32[]{:S(2)}) %all-to-all-start.2) | async-done | bytes 524320 | tf_op jit(solution)/shard_map/all_to_all | solution.py:86
  118.0 3.2 %collective-permute-start.10 = (bf16[256,1024]{1,0:T(8,128)(2,1)S(1)}, bf16[256,1024]{1,0:T(8,128)(2,1)}, u32[]{:S(2)}, u32[]{:S(2)}) collective-permute-start(bf16[256,1024]{1,0:T(8,128)(2,1)S(1)} %bitcast.16), channel_id=1, source_target_pairs={{0,1},{1,0},{2,3},{3,2},{4,5},{5,4},{6,7},{7,6},{8,9},{9,8},{10,11... | collective-permute-start | bytes 1572872 | tf_op jit(solution)/shard_map/ppermute | solution.py:30
  122.9 1.8 %fusion.1 = bf16[256,1024]{1,0:T(8,128)(2,1)S(1)} fusion(f32[256,1024]{1,0:T(8,128)S(1)} %fusion.15, bf16[1024,512]{1,0:T(8,128)(2,1)} %collective-permute-done.3, bf16[256,1024]{1,0:T(8,128)(2,1)S(1)} %bitcast.18), kind=kOutput, calls=%fused_computation.4 | convolution fusion | flops 268959744 | bytes 2883584 | tf_op jit(solution)/shard_map/dot_general | solution.py:92
  126.2 1.7 fusion
  129.4 2.4 %maximum_bitcast_fusion = bf16[4,4,2,64,2,128]{5,4,3,2,1,0:T(2,128)(2,1)S(1)} fusion(bf16[1,4,64,4,2,128]{5,0,2,4,1,3:T(2,128)(2,1)S(1)} %copy.12, bf16[1,4,64,4,2,128]{5,0,2,4,1,3:T(2,128)(2,1)S(1)} %copy.11), kind=kLoop, calls=%fused_computation.9 | loop fusion | flops 2097152 | bytes 2097152 | tf_op jit(solution)/shard_map/transpose | solution.py:96
  133.4 8.1 %all-to-all-start.3 = ((bf16[32,64,256]{2,1,0:T(8,128)(2,1)}), bf16[32,64,256]{2,1,0:T(8,128)(2,1)S(1)}, u32[]{:S(2)}, u32[]{:S(2)}) async-start(bf16[32,64,256]{2,1,0:T(8,128)(2,1)} %all_to_all.27), calls=%async_computation.3 | async-start | bytes 2097152 | tf_op jit(solution)/shard_map/all_to_all | solution.py:97
  142.6 1.9 %collective-permute-start.11 = (bf16[512,1024]{1,0:T(8,128)(2,1)S(1)}, bf16[512,1024]{1,0:T(8,128)(2,1)S(1)}, u32[]{:S(2)}, u32[]{:S(2)}) collective-permute-start(bf16[512,1024]{1,0:T(8,128)(2,1)S(1)} %pad_maximum_fusion), channel_id=1, source_target_pairs={{0,64},{64,0},{1,65},{65,1},{2,66},{66,2},{3,67},{67,3},{4,68},{68... | collective-permute-start | bytes 3145736 | tf_op jit(solution)/shard_map/ppermute | solution.py:26
  145.7 2.4 %collective-permute-start.12 = (bf16[512,512]{1,0:T(8,128)(2,1)S(1)}, bf16[512,512]{1,0:T(8,128)(2,1)S(1)}, u32[]{:S(2)}, u32[]{:S(2)}) collective-permute-start(bf16[512,512]{1,0:T(8,128)(2,1)S(1)} %pad_maximum_fusion.2), channel_id=1, source_target_pairs={{0,64},{64,0},{1,65},{65,1},{2,66},{66,2},{3,67},{67,3},{4,68},{68... | collective-permute-start | bytes 1572872 | tf_op jit(solution)/shard_map/ppermute | solution.py:26
  148.1 2.7 %collective-permute-start.4 = (bf16[64,256]{1,0:T(8,128)(2,1)S(1)}, bf16[64,256]{1,0:T(8,128)(2,1)S(1)}, u32[]{:S(2)}, u32[]{:S(2)}) collective-permute-start(bf16[64,256]{1,0:T(8,128)(2,1)S(1)} %get-tuple-element.26), channel_id=1, source_target_pairs={{0,1},{1,0},{2,3},{3,2},{4,5},{5,4},{6,7},{7,6},{8,9},{9,8},{10,11... | collective-permute-start | bytes 98312 | tf_op jit(solution)/shard_map/ppermute | solution.py:30
  150.8 3.1 %collective-permute-done.4 = bf16[64,256]{1,0:T(8,128)(2,1)S(1)} collective-permute-done((bf16[64,256]{1,0:T(8,128)(2,1)S(1)}, bf16[64,256]{1,0:T(8,128)(2,1)S(1)}, u32[]{:S(2)}, u32[]{:S(2)}) %collective-permute-start.4) | collective-permute-done | bytes 32800 | tf_op jit(solution)/shard_map/ppermute | solution.py:30
  154.0 1.9 %collective-permute-start.5 = (bf16[128,256]{1,0:T(8,128)(2,1)S(1)}, bf16[128,256]{1,0:T(8,128)(2,1)S(1)}, u32[]{:S(2)}, u32[]{:S(2)}) collective-permute-start(bf16[128,256]{1,0:T(8,128)(2,1)S(1)} %maximum_select_fusion), channel_id=1, source_target_pairs={{0,0},{1,1},{2,128},{3,129},{4,256},{5,257},{6,384},{7,385},{64,64... | collective-permute-start | bytes 196616 | tf_op jit(solution)/shard_map/ppermute | solution.py:101
  155.9 9.9 %collective-permute-done.5 = bf16[128,256]{1,0:T(8,128)(2,1)S(1)} collective-permute-done((bf16[128,256]{1,0:T(8,128)(2,1)S(1)}, bf16[128,256]{1,0:T(8,128)(2,1)S(1)}, u32[]{:S(2)}, u32[]{:S(2)}) %collective-permute-start.5) | collective-permute-done | bytes 65568 | tf_op jit(solution)/shard_map/ppermute | solution.py:101
  166.6 1.8 %add_convert_fusion = bf16[1024,512]{1,0:T(8,128)(2,1)S(1)} fusion(f32[1024,512]{1,0:T(8,128)S(1)} %fusion.33, bf16[256,512]{1,0:T(8,128)(2,1)S(1)} %get-tuple-element.10, bf16[256,512]{1,0:T(8,128)(2,1)S(1)} %get-tuple-element.8, bf16[256,1024]{1,0:T(8,128)(2,1)} %collective-permute-done.9, bf16[256,1024]{1,0:T(8,128)(2,1)S(1)} %copy-done.1), kind=kOutput, calls=%fused_computation | convolution fusion | flops 541065216 | bytes 4718592 | tf_op jit(solution)/shard_map/dot_general | solution.py:107
  168.6 2.9 %collective-permute-start.8 = (bf16[64,128]{1,0:T(8,128)(2,1)S(1)}, bf16[64,128]{1,0:T(8,128)(2,1)S(1)}, u32[]{:S(2)}, u32[]{:S(2)}) collective-permute-start(bf16[64,128]{1,0:T(8,128)(2,1)S(1)} %get-tuple-element.28), channel_id=1, source_target_pairs={{0,1},{1,0},{2,3},{3,2},{4,5},{5,4},{6,7},{7,6},{8,9},{9,8},{10,11... | collective-permute-start | bytes 49160 | tf_op jit(solution)/shard_map/ppermute | solution.py:30
  172.5 1.7 collective-permute-done.8
  (56 shorter events, 23.0 us)
Async XLA Ops:
  0.6 19.2 %copy-start.2 = (bf16[1024,256]{1,0:T(8,128)(2,1)S(1)}, bf16[1024,256]{1,0:T(8,128)(2,1)}, u32[]{:S(2)}) copy-start(bf16[1024,256]{1,0:T(8,128)(2,1)} %param.5) | copy-start | bytes 1572868
  1.4 5.6 %collective-permute-start = (bf16[64,128]{1,0:T(8,128)(2,1)S(1)}, bf16[64,128]{1,0:T(8,128)(2,1)S(1)}, u32[]{:S(2)}, u32[]{:S(2)}) collective-permute-start(bf16[64,128]{1,0:T(8,128)(2,1)S(1)} %get-tuple-element.30), channel_id=1, source_target_pairs={{0,1},{1,0},{2,3},{3,2},{4,5},{5,4},{6,7},{7,6},{8,9},{9,8},{10,11... | collective-permute-start | bytes 49160 | tf_op jit(solution)/shard_map/ppermute | solution.py:30
  7.1 12.8 %copy-start.3 = (bf16[1024,256]{1,0:T(8,128)(2,1)S(1)}, bf16[1024,256]{1,0:T(8,128)(2,1)}, u32[]{:S(2)}) copy-start(bf16[1024,256]{1,0:T(8,128)(2,1)} %param.6) | copy-start | bytes 1572868
  8.2 38.9 %all-to-all-start = ((bf16[32,64,256]{2,1,0:T(8,128)(2,1)}), bf16[32,64,256]{2,1,0:T(8,128)(2,1)S(1)}, u32[]{:S(2)}, u32[]{:S(2)}) async-start(bf16[32,64,256]{2,1,0:T(8,128)(2,1)} %tile.4), calls=%async_computation | async-start | bytes 2097152 | tf_op jit(solution)/shard_map/all_to_all | solution.py:49
  19.9 25.2 %collective-permute-start.1 = (bf16[1024,512]{1,0:T(8,128)(2,1)S(1)}, bf16[1024,512]{1,0:T(8,128)(2,1)}, u32[]{:S(2)}, u32[]{:S(2)}) collective-permute-start(bf16[1024,512]{1,0:T(8,128)(2,1)S(1)} %constant_dynamic-update-slice_fusion), channel_id=1, source_target_pairs={{0,1},{1,0},{2,3},{3,2},{4,5},{5,4},{6,7},{7,6},{8,9},{9,8},{10,11... | collective-permute-start | bytes 3145736 | tf_op jit(solution)/shard_map/ppermute | solution.py:30
  23.4 30.9 %collective-permute-start.2 = (bf16[1024,512]{1,0:T(8,128)(2,1)S(1)}, bf16[1024,512]{1,0:T(8,128)(2,1)}, u32[]{:S(2)}, u32[]{:S(2)}) collective-permute-start(bf16[1024,512]{1,0:T(8,128)(2,1)S(1)} %constant_dynamic-update-slice_fusion), channel_id=1, source_target_pairs={{0,64},{64,0},{1,65},{65,1},{2,66},{66,2},{3,67},{67,3},{4,68},{68... | collective-permute-start | bytes 3145736 | tf_op jit(solution)/shard_map/ppermute | solution.py:26
  45.1 12.5 %collective-permute-start.3 = (bf16[1024,512]{1,0:T(8,128)(2,1)}, bf16[1024,512]{1,0:T(8,128)(2,1)}, u32[]{:S(2)}, u32[]{:S(2)}) collective-permute-start(bf16[1024,512]{1,0:T(8,128)(2,1)} %collective-permute-done.1), channel_id=1, source_target_pairs={{0,64},{64,0},{1,65},{65,1},{2,66},{66,2},{3,67},{67,3},{4,68},{68... | collective-permute-start | bytes 3145736 | tf_op jit(solution)/shard_map/ppermute | solution.py:26
  57.6 9.7 %copy-start.4 = (bf16[128,256]{1,0:T(8,128)(2,1)S(1)}, bf16[128,256]{1,0:T(8,128)(2,1)}, u32[]{:S(2)}) copy-start(bf16[128,256]{1,0:T(8,128)(2,1)} %param.7) | copy-start | bytes 196612
  60.2 29.1 %all-to-all-start.1 = ((bf16[4,64,1024]{2,1,0:T(8,128)(2,1)}), bf16[4,64,1024]{2,1,0:T(8,128)(2,1)S(1)}, u32[]{:S(2)}, u32[]{:S(2)}) async-start(bf16[4,64,1024]{2,1,0:T(8,128)(2,1)} %bitcast.1), calls=%async_computation.1 | async-start | bytes 1048576 | tf_op jit(solution)/shard_map/all_to_all | solution.py:73
  67.3 19.5 %collective-permute-start.6 = (bf16[128,256]{1,0:T(8,128)(2,1)S(1)}, bf16[128,256]{1,0:T(8,128)(2,1)S(1)}, u32[]{:S(2)}, u32[]{:S(2)}) collective-permute-start(bf16[128,256]{1,0:T(8,128)(2,1)S(1)} %copy-done.4), channel_id=1, source_target_pairs={{0,0},{1,1},{128,2},{129,3},{256,4},{257,5},{384,6},{385,7},{64,64... | collective-permute-start | bytes 196616 | tf_op jit(solution)/shard_map/ppermute | solution.py:54
  86.8 5.8 %collective-permute-start.7 = (bf16[64,256]{1,0:T(8,128)(2,1)S(1)}, bf16[64,256]{1,0:T(8,128)(2,1)S(1)}, u32[]{:S(2)}, u32[]{:S(2)}) collective-permute-start(bf16[64,256]{1,0:T(8,128)(2,1)S(1)} %get-tuple-element.23), channel_id=1, source_target_pairs={{0,1},{1,0},{2,3},{3,2},{4,5},{5,4},{6,7},{7,6},{8,9},{9,8},{10,11... | collective-permute-start | bytes 98312 | tf_op jit(solution)/shard_map/ppermute | solution.py:30
  93.6 22.9 %all-to-all-start.2 = ((bf16[4,64,1024]{2,1,0:T(8,128)(2,1)}), bf16[4,64,1024]{2,1,0:T(8,128)(2,1)S(1)}, u32[]{:S(2)}, u32[]{:S(2)}) async-start(bf16[4,64,1024]{2,1,0:T(8,128)(2,1)} %tile.5), calls=%async_computation.2 | async-start | bytes 1048576 | tf_op jit(solution)/shard_map/all_to_all | solution.py:86
  99.4 42.1 %collective-permute-start.9 = (bf16[256,1024]{1,0:T(8,128)(2,1)}, bf16[256,1024]{1,0:T(8,128)(2,1)}, u32[]{:S(2)}, u32[]{:S(2)}) collective-permute-start(bf16[256,1024]{1,0:T(8,128)(2,1)} %get-tuple-element.7), channel_id=1, source_target_pairs={{0,1},{1,0},{2,3},{3,2},{4,5},{5,4},{6,7},{7,6},{8,9},{9,8},{10,11... | collective-permute-start | bytes 1572872 | tf_op jit(solution)/shard_map/ppermute | solution.py:30
  118.0 26.6 %collective-permute-start.10 = (bf16[256,1024]{1,0:T(8,128)(2,1)S(1)}, bf16[256,1024]{1,0:T(8,128)(2,1)}, u32[]{:S(2)}, u32[]{:S(2)}) collective-permute-start(bf16[256,1024]{1,0:T(8,128)(2,1)S(1)} %bitcast.16), channel_id=1, source_target_pairs={{0,1},{1,0},{2,3},{3,2},{4,5},{5,4},{6,7},{7,6},{8,9},{9,8},{10,11... | collective-permute-start | bytes 1572872 | tf_op jit(solution)/shard_map/ppermute | solution.py:30
  122.9 3.3 %copy-start = (f32[256,1024]{1,0:T(8,128)S(1)}, f32[256,1024]{1,0:T(8,128)}, u32[]{:S(2)}) copy-start(f32[256,1024]{1,0:T(8,128)} %fusion.17) | copy-start | bytes 3145732
  131.9 9.6 %copy-start.1 = (bf16[256,1024]{1,0:T(8,128)(2,1)S(1)}, bf16[256,1024]{1,0:T(8,128)(2,1)}, u32[]{:S(2)}) copy-start(bf16[256,1024]{1,0:T(8,128)(2,1)} %get-tuple-element.6) | copy-start | bytes 1572868
  133.4 35.0 %all-to-all-start.3 = ((bf16[32,64,256]{2,1,0:T(8,128)(2,1)}), bf16[32,64,256]{2,1,0:T(8,128)(2,1)S(1)}, u32[]{:S(2)}, u32[]{:S(2)}) async-start(bf16[32,64,256]{2,1,0:T(8,128)(2,1)} %all_to_all.27), calls=%async_computation.3 | async-start | bytes 2097152 | tf_op jit(solution)/shard_map/all_to_all | solution.py:97
  142.6 23.2 %collective-permute-start.11 = (bf16[512,1024]{1,0:T(8,128)(2,1)S(1)}, bf16[512,1024]{1,0:T(8,128)(2,1)S(1)}, u32[]{:S(2)}, u32[]{:S(2)}) collective-permute-start(bf16[512,1024]{1,0:T(8,128)(2,1)S(1)} %pad_maximum_fusion), channel_id=1, source_target_pairs={{0,64},{64,0},{1,65},{65,1},{2,66},{66,2},{3,67},{67,3},{4,68},{68... | collective-permute-start | bytes 3145736 | tf_op jit(solution)/shard_map/ppermute | solution.py:26
  145.7 20.1 %collective-permute-start.12 = (bf16[512,512]{1,0:T(8,128)(2,1)S(1)}, bf16[512,512]{1,0:T(8,128)(2,1)S(1)}, u32[]{:S(2)}, u32[]{:S(2)}) collective-permute-start(bf16[512,512]{1,0:T(8,128)(2,1)S(1)} %pad_maximum_fusion.2), channel_id=1, source_target_pairs={{0,64},{64,0},{1,65},{65,1},{2,66},{66,2},{3,67},{67,3},{4,68},{68... | collective-permute-start | bytes 1572872 | tf_op jit(solution)/shard_map/ppermute | solution.py:26
  148.1 5.8 %collective-permute-start.4 = (bf16[64,256]{1,0:T(8,128)(2,1)S(1)}, bf16[64,256]{1,0:T(8,128)(2,1)S(1)}, u32[]{:S(2)}, u32[]{:S(2)}) collective-permute-start(bf16[64,256]{1,0:T(8,128)(2,1)S(1)} %get-tuple-element.26), channel_id=1, source_target_pairs={{0,1},{1,0},{2,3},{3,2},{4,5},{5,4},{6,7},{7,6},{8,9},{9,8},{10,11... | collective-permute-start | bytes 98312 | tf_op jit(solution)/shard_map/ppermute | solution.py:30
  154.0 11.9 %collective-permute-start.5 = (bf16[128,256]{1,0:T(8,128)(2,1)S(1)}, bf16[128,256]{1,0:T(8,128)(2,1)S(1)}, u32[]{:S(2)}, u32[]{:S(2)}) collective-permute-start(bf16[128,256]{1,0:T(8,128)(2,1)S(1)} %maximum_select_fusion), channel_id=1, source_target_pairs={{0,0},{1,1},{2,128},{3,129},{4,256},{5,257},{6,384},{7,385},{64,64... | collective-permute-start | bytes 196616 | tf_op jit(solution)/shard_map/ppermute | solution.py:101
  168.6 5.6 %collective-permute-start.8 = (bf16[64,128]{1,0:T(8,128)(2,1)S(1)}, bf16[64,128]{1,0:T(8,128)(2,1)S(1)}, u32[]{:S(2)}, u32[]{:S(2)}) collective-permute-start(bf16[64,128]{1,0:T(8,128)(2,1)S(1)} %get-tuple-element.28), channel_id=1, source_target_pairs={{0,1},{1,0},{2,3},{3,2},{4,5},{5,4},{6,7},{7,6},{8,9},{9,8},{10,11... | collective-permute-start | bytes 49160 | tf_op jit(solution)/shard_map/ppermute | solution.py:30

commit v3 on v2

v3 whole, which is shorter than its diff:
```python
import jax
import jax.numpy as jnp
from jax import lax
from jax.experimental import pallas as pl
from jax.experimental.pallas import tpu as pltpu
from jax.sharding import Mesh, PartitionSpec as P

PLANE = ("x", "zl", "zh")
F32 = jnp.float32
BF16 = jnp.bfloat16
LAST = (((1,), (1,)), ((), ()))
ROWS = (((0,), (0,)), ((), ()))


def regroup():
    pairs = []
    for zl in range(4):
        for co in range(2):
            for q in range(4):
                for p in range(2):
                    work = (zl * 2 + co) * 8 + 2 * q + p
                    home = (q * 2 + co) * 8 + 2 * zl + p
                    pairs.append((work, home))
    return pairs


def swap_cores(value):
    return lax.ppermute(value, "co", [(0, 1), (1, 0)])


def swap_pair(value):
    return lax.ppermute(value, "yp", [(0, 1), (1, 0)])


def forward_kernel(side_ref, tiles, own, own_pair, other, other_pair, parts, near, far):
    side = side_ref[0]
    for x in range(4):
        for zl in range(4):
            for zh in range(2):
                row, column = slice(64 * zl, 64 * zl + 64), slice(128 * (2 * x + zh), 128 * (2 * x + zh + 1))
                near[row, column] = tiles[x, zl, zh, side]
                far[row, column] = tiles[x, zl, zh, 1 - side]
    for at, (first, second) in enumerate(((own, own_pair), (other, other_pair))):
        total = jnp.dot(near[...], first[...], preferred_element_type=F32)
        total += jnp.dot(far[...], second[...], preferred_element_type=F32)
        parts[:, 512 * at : 512 * (at + 1)] = total.astype(BF16)


def backward_kernel(side_ref, grads, own, own_pair, other, other_pair, blocks):
    side = side_ref[0]
    for place, first, second in ((side, own, other), (1 - side, own_pair, other_pair)):
        for x in range(4):
            rows = slice(256 * x, 256 * (x + 1))
            total = lax.dot_general(grads[:, :512], first[rows], LAST, preferred_element_type=F32)
            total += lax.dot_general(grads[:, 512:], second[rows], LAST, preferred_element_type=F32)
            total = total.astype(BF16)
            for zl in range(4):
                for zh in range(2):
                    tile = total[64 * zl : 64 * zl + 64, 128 * zh : 128 * zh + 128]
                    blocks[x, zl, zh, place] = tile


def call(kernel, out_shapes, inputs):
    vmem = pl.BlockSpec(memory_space=pltpu.VMEM)
    return pl.pallas_call(
        kernel,
        out_shape=[jax.ShapeDtypeStruct(shape, BF16) for shape in out_shapes],
        in_specs=[pl.BlockSpec(memory_space=pltpu.SMEM)] + [vmem] * (len(inputs) - 1),
        out_specs=[vmem] * len(out_shapes),
        compiler_params=pltpu.CompilerParams(vmem_limit_bytes=40 * 1024 * 1024),
    )(*inputs)


def body(tokens, gate_weight, up_weight, hidden_grad):
    core, side = lax.axis_index("co"), lax.axis_index("yp")
    low, own_first = side == 0, side == core
    side_word = side.astype(jnp.int32).reshape(1)
    perm = regroup()
    everyone = ("zl", "co", "yq", "yp")

    copies, gate_weight, up_weight, hidden_grad = lax.optimization_barrier(
        (jnp.tile(tokens, (32, 1)), gate_weight, up_weight, hidden_grad)
    )
    tiles = lax.all_to_all(copies, PLANE + ("yp",), 0, 0, tiled=True)
    own = jnp.concatenate([gate_weight, up_weight], axis=1)
    own_pair = swap_pair(own)
    other = swap_cores(own)
    other_pair = swap_cores(own_pair)
    weights = (own, own_pair, other, other_pair)
    upstream = lax.ppermute(hidden_grad, everyone, [(home, work) for work, home in perm])
    kept = jnp.where(low, upstream[:64], upstream[64:])
    received = swap_pair(jnp.where(low, upstream[64:], upstream[:64]))
    upstream = jnp.where(
        own_first,
        jnp.concatenate([kept, received], axis=1),
        jnp.concatenate([received, kept], axis=1),
    ).astype(F32)

    parts, near_rows, far_rows = call(
        forward_kernel,
        [(256, 1024)] * 3,
        (side_word, tiles.reshape(4, 4, 2, 2, 64, 128)) + weights,
    )
    parts = lax.all_to_all(parts, "yq", 0, 0, tiled=True)
    sums = jnp.sum(parts.reshape(4, 64, 1024).astype(F32), axis=0)
    gate_sum = jnp.concatenate([sums[:, :256], sums[:, 512:768]], axis=1)
    up_sum = jnp.concatenate([sums[:, 256:512], sums[:, 768:]], axis=1)
    sigmoid_gate = jax.nn.sigmoid(gate_sum)
    activated = gate_sum * sigmoid_gate
    hidden = (activated * up_sum).astype(BF16)
    gate_grad = upstream * up_sum * sigmoid_gate * (1.0 + gate_sum * (1.0 - sigmoid_gate))
    up_grad = upstream * activated
    gate_grad, up_grad = gate_grad.astype(BF16), up_grad.astype(BF16)
    grads = jnp.concatenate(
        [gate_grad[:, :256], up_grad[:, :256], gate_grad[:, 256:], up_grad[:, 256:]], axis=1
    )
    grads = lax.all_to_all(jnp.tile(grads, (4, 1)), "yq", 0, 0, tiled=True)

    grads, far_rows = lax.optimization_barrier((grads, far_rows))
    (blocks,) = call(backward_kernel, [(4, 4, 2, 2, 64, 128)], (side_word, grads) + weights)
    blocks = lax.all_to_all(
        blocks.reshape(64 * 64, 128), PLANE + ("yp",), 0, 0, tiled=True
    )

    kept = jnp.where(own_first, hidden[:, :256], hidden[:, 256:])
    received = swap_pair(jnp.where(own_first, hidden[:, 256:], hidden[:, :256]))
    hidden = jnp.where(low, jnp.concatenate([kept, received]), jnp.concatenate([received, kept]))
    hidden = lax.ppermute(hidden, everyone, perm)

    pair_grads = swap_pair(grads)
    pair_rows = swap_pair(far_rows)
    wgrad = sum(
        lax.dot_general(left, right, ROWS, preferred_element_type=F32)
        for left, right in (
            (near_rows, grads[:, :512]),
            (swap_cores(near_rows), swap_cores(grads[:, 512:])),
            (pair_rows, pair_grads[:, :512]),
            (swap_cores(pair_rows), swap_cores(pair_grads[:, 512:])),
        )
    )
    wgrad = wgrad.astype(BF16)
    input_grad = jnp.sum(blocks.reshape(32, 128, 128).astype(F32), axis=0).astype(BF16)
    return hidden, input_grad, wgrad[:, :256], wgrad[:, 256:]


def solution(mesh):
    axes = ("zl", "co", "x", "zh", "yq", "yp")
    fine = Mesh(mesh.devices.reshape(4, 2, 4, 2, 4, 2), axes)
    gx, gy, gz = ("zl", "co"), ("x", "zh"), ("yq", "yp")
    in_specs = (P(gx, gz + gy), P(gz, gy + gx), P(gz, gy + gx), P(gx, gy + gz))
    out_specs = (P(gx, gy + gz), P(gx, gz + gy), P(gz, gy + gx), P(gz, gy + gx))
    return jax.shard_map(body, mesh=fine, in_specs=in_specs, out_specs=out_specs, check_vma=False)
```

time: 177 us -> 172 us (0.972)
  the two profiles are of different devices: /device:TPU:128 before, /device:TPU:41 now
where the time goes in v3:
time: 172 us; the launch traced here: 171 us
  starting transfers between devices  79.3 us (46%)
  waiting for transfers between devices  59.9 us (35%)
  blocking collectives  14.4 us (8%)
  local copies, waits for them, and re-layouts  7.33 us (4%)
  Pallas kernels  6.72 us (4%)
  matrix products  1.9 us (1%)
    ppermute x5, waiting for transfers between devices, swap_pair(): return lax.ppermute(value, 'yp', [(0, 1), (1, 0)])  25.3 us
    ppermute x6, starting transfers between devices, swap_cores(): return lax.ppermute(value, 'co', [(0, 1), (1, 0)])  23.6 us
    all_to_all x1, waiting for transfers between devices, body(): tiles = lax.all_to_all(copies, PLANE + ('yp',), 0, 0, tiled=True)  17.6 us
    all_to_all x1, blocking collectives, body(): grads = lax.all_to_all(jnp.tile(grads, (4, 1)), 'yq', 0, 0, tiled=True)  14.4 us
    all_to_all x1, starting transfers between devices, body(): tiles = lax.all_to_all(copies, PLANE + ('yp',), 0, 0, tiled=True)  14.2 us
    all_to_all x1, starting transfers between devices, body(): lax.all_to_all(blocks.reshape(64 * 64, 128), PLANE + ('yp',), 0, 0, tiled...  13.5 us
    ppermute x5, starting transfers between devices, swap_pair(): return lax.ppermute(value, 'yp', [(0, 1), (1, 0)])  12.7 us
    ppermute x1, waiting for transfers between devices, body(): lax.ppermute(hidden_grad, everyone, [(home, work) for work, home in perm])  10.3 us
  transfers between devices with their start and end apart: 16, of which 8 were waited for; matrix products, arithmetic and copies ran while one was open for 2% of the time, Pallas kernels for 0%

profile of v3, /device:TPU:41, one launch (start us, length us, event | category | flops | bytes accessed | tf_op | source)
XLA Modules:
  0.0 171.5 jit_solution(17844968101722532256)
XLA Ops:
  0.6 2.0 %tile.6 = bf16[32,128,128]{2,1,0:T(8,128)(2,1)} broadcast(bf16[128,128]{1,0:T(8,128)(2,1)} %param.4), dimensions={1,2} | broadcast | bytes 1081344 | tf_op jit(solution)/shard_map/tile | solution.py:82
  2.7 1.1 constant_dynamic-update-slice_fusion.1
  3.8 3.0 %collective-permute-start = (bf16[1024,512]{1,0:T(8,128)(2,1)S(1)}, bf16[1024,512]{1,0:T(8,128)(2,1)S(1)}, u32[]{:S(2)}, u32[]{:S(2)}) collective-permute-start(bf16[1024,512]{1,0:T(8,128)(2,1)S(1)} %constant_dynamic-update-slice_fusion.own), channel_id=1, source_target_pairs={{0,1},{1,0},{2,3},{3,2},{4,5},{5,4},{6,7},{7,6},{8,9},{9,8},{10,11... | collective-permute-start | bytes 3145736 | tf_op jit(solution)/shard_map/ppermute | solution.py:32
  6.8 14.2 %all-to-all-start = ((bf16[64,64,128]{2,1,0:T(8,128)(2,1)}), bf16[64,64,128]{2,1,0:T(8,128)(2,1)S(1)}, u32[]{:S(2)}, u32[]{:S(2)}) async-start(bf16[64,64,128]{2,1,0:T(8,128)(2,1)} %bitcast.23), calls=%async_computation | async-start | bytes 2097152 | tf_op jit(solution)/shard_map/all_to_all | solution.py:84
  21.1 3.4 %collective-permute-start.1 = (bf16[1024,512]{1,0:T(8,128)(2,1)S(1)}, bf16[1024,512]{1,0:T(8,128)(2,1)}, u32[]{:S(2)}, u32[]{:S(2)}) collective-permute-start(bf16[1024,512]{1,0:T(8,128)(2,1)S(1)} %constant_dynamic-update-slice_fusion.own), channel_id=1, source_target_pairs={{0,64},{64,0},{1,65},{65,1},{2,66},{66,2},{3,67},{67,3},{4,68},{68... | collective-permute-start | bytes 3145736 | tf_op jit(solution)/shard_map/ppermute | solution.py:28
  24.5 5.3 %collective-permute-done.own_pair = bf16[1024,512]{1,0:T(8,128)(2,1)S(1)} collective-permute-done((bf16[1024,512]{1,0:T(8,128)(2,1)S(1)}, bf16[1024,512]{1,0:T(8,128)(2,1)S(1)}, u32[]{:S(2)}, u32[]{:S(2)}) %collective-permute-start) | collective-permute-done | bytes 1048608 | tf_op jit(solution)/shard_map/ppermute | solution.py:32
  29.7 4.6 %collective-permute-start.2 = (bf16[1024,512]{1,0:T(8,128)(2,1)S(1)}, bf16[1024,512]{1,0:T(8,128)(2,1)}, u32[]{:S(2)}, u32[]{:S(2)}) collective-permute-start(bf16[1024,512]{1,0:T(8,128)(2,1)S(1)} %collective-permute-done.own_pair), channel_id=1, source_target_pairs={{0,64},{64,0},{1,65},{65,1},{2,66},{66,2},{3,67},{67,3},{4,68},{68... | collective-permute-start | bytes 3145736 | tf_op jit(solution)/shard_map/ppermute | solution.py:28
  34.4 17.6 %all-to-all-done = bf16[64,64,128]{2,1,0:T(8,128)(2,1)S(1)} async-done(((bf16[64,64,128]{2,1,0:T(8,128)(2,1)}), bf16[64,64,128]{2,1,0:T(8,128)(2,1)S(1)}, u32[]{:S(2)}, u32[]{:S(2)}) %all-to-all-start) | async-done | bytes 1048608 | tf_op jit(solution)/shard_map/all_to_all | solution.py:84
  51.9 2.9 %shard_map.75 = (bf16[256,1024]{1,0:T(8,128)(2,1)S(1)}, bf16[256,1024]{1,0:T(8,128)(2,1)S(1)}, bf16[256,1024]{1,0:T(8,128)(2,1)S(1)}) custom-call(s32[1]{0:T(128)} %bitcast.side_ref, bf16[4,4,2,2,64,128]{5,4,3,2,1,0:T(8,128)(2,1)S(1)} %bitcast.20, bf16[1024,512]{1,0:T(8,128)(2,1)S(1)} %constant_dynamic-update-slice_fusion.own, ...), custom_call_target="tpu_custom_call" | custom-call | tf_op jit(solution)/shard_map/pallas_call | solution.py:65
  54.8 0.8 copy-done.1
  55.6 0.8 copy-done.3
  56.4 0.8 copy-done
  57.2 6.6 %all-to-all-start.1 = ((bf16[4,64,1024]{2,1,0:T(8,128)(2,1)}), bf16[4,64,1024]{2,1,0:T(8,128)(2,1)S(1)}, u32[]{:S(2)}, u32[]{:S(2)}) async-start(bf16[4,64,1024]{2,1,0:T(8,128)(2,1)} %bitcast.21), calls=%async_computation.1 | async-start | bytes 1048576 | tf_op jit(solution)/shard_map/all_to_all | solution.py:104
  63.9 3.5 %collective-permute-start.5 = (bf16[128,256]{1,0:T(8,128)(2,1)S(1)}, bf16[128,256]{1,0:T(8,128)(2,1)S(1)}, u32[]{:S(2)}, u32[]{:S(2)}) collective-permute-start(bf16[128,256]{1,0:T(8,128)(2,1)S(1)} %copy-done.6), channel_id=1, source_target_pairs={{0,0},{1,1},{128,2},{129,3},{256,4},{257,5},{384,6},{385,7},{64,64... | collective-permute-start | bytes 196616 | tf_op jit(solution)/shard_map/ppermute | solution.py:90
  67.3 10.3 %collective-permute-done.5 = bf16[128,256]{1,0:T(8,128)(2,1)S(1)} collective-permute-done((bf16[128,256]{1,0:T(8,128)(2,1)S(1)}, bf16[128,256]{1,0:T(8,128)(2,1)S(1)}, u32[]{:S(2)}, u32[]{:S(2)}) %collective-permute-start.5) | collective-permute-done | bytes 65568 | tf_op jit(solution)/shard_map/ppermute | solution.py:90
  77.6 1.9 %collective-permute-start.6 = (bf16[64,256]{1,0:T(8,128)(2,1)S(1)}, bf16[64,256]{1,0:T(8,128)(2,1)S(1)}, u32[]{:S(2)}, u32[]{:S(2)}) collective-permute-start(bf16[64,256]{1,0:T(8,128)(2,1)S(1)} %get-tuple-element.35), channel_id=1, source_target_pairs={{0,1},{1,0},{2,3},{3,2},{4,5},{5,4},{6,7},{7,6},{8,9},{9,8},{10,11... | collective-permute-start | bytes 98312 | tf_op jit(solution)/shard_map/ppermute | solution.py:32
  79.7 2.6 %collective-permute-done.6 = bf16[64,256]{1,0:T(8,128)(2,1)S(1)} collective-permute-done((bf16[64,256]{1,0:T(8,128)(2,1)S(1)}, bf16[64,256]{1,0:T(8,128)(2,1)S(1)}, u32[]{:S(2)}, u32[]{:S(2)}) %collective-permute-start.6) | collective-permute-done | bytes 32800 | tf_op jit(solution)/shard_map/ppermute | solution.py:32
  82.5 14.4 %all_to_all.36 = bf16[4,64,1024]{2,1,0:T(8,128)(2,1)S(1)} all-to-all(bf16[4,64,1024]{2,1,0:T(8,128)(2,1)S(1)} %tile.8), channel_id=1, replica_groups=mesh['zl'=4,'co'=2,'x'=4,'zh'=2,'yq'=4,'yp'=2] {'yq'}, dimensions={0} | all-to-all | bytes 1048576 | tf_op jit(solution)/shard_map/all_to_all | solution.py:117
  96.9 3.8 %shard_map.76 = bf16[4,4,2,2,64,128]{5,4,3,2,1,0:T(8,128)(2,1)} custom-call(s32[1]{0:T(128)} %bitcast.side_ref, bf16[256,1024]{1,0:T(8,128)(2,1)S(1)} %bitcast.16, bf16[1024,512]{1,0:T(8,128)(2,1)S(1)} %constant_dynamic-update-slice_fusion.own, bf16[1024,512]{1,0:T(8,128)(2,1)S(1)} %collective-permute-done.own_pair, ...), custom_call_target="tpu_custom_call" | custom-call | tf_op jit(solution)/shard_map/pallas_call | solution.py:65
  100.7 13.5 %all-to-all-start.3 = ((bf16[64,64,128]{2,1,0:T(8,128)(2,1)}), bf16[64,64,128]{2,1,0:T(8,128)(2,1)S(1)}, u32[]{:S(2)}, u32[]{:S(2)}) async-start(bf16[64,64,128]{2,1,0:T(8,128)(2,1)} %bitcast.6), calls=%async_computation.3 | async-start | bytes 2097152 | tf_op jit(solution)/shard_map/all_to_all | solution.py:121
  114.3 3.2 %collective-permute-start.7 = (bf16[256,1024]{1,0:T(8,128)(2,1)S(1)}, bf16[256,1024]{1,0:T(8,128)(2,1)S(1)}, u32[]{:S(2)}, u32[]{:S(2)}) collective-permute-start(bf16[256,1024]{1,0:T(8,128)(2,1)S(1)} %copy-done.2), channel_id=1, source_target_pairs={{0,64},{64,0},{1,65},{65,1},{2,66},{66,2},{3,67},{67,3},{4,68},{68... | collective-permute-start | bytes 1572872 | tf_op jit(solution)/shard_map/ppermute | solution.py:28
  117.5 2.1 %collective-permute-start.9 = (bf16[256,1024]{1,0:T(8,128)(2,1)S(1)}, bf16[256,1024]{1,0:T(8,128)(2,1)S(1)}, u32[]{:S(2)}, u32[]{:S(2)}) collective-permute-start(bf16[256,1024]{1,0:T(8,128)(2,1)S(1)} %copy-done.4), channel_id=1, source_target_pairs={{0,1},{1,0},{2,3},{3,2},{4,5},{5,4},{6,7},{7,6},{8,9},{9,8},{10,11... | collective-permute-start | bytes 1572872 | tf_op jit(solution)/shard_map/ppermute | solution.py:32
  119.6 3.2 %collective-permute-start.3 = (bf16[64,256]{1,0:T(8,128)(2,1)S(1)}, bf16[64,256]{1,0:T(8,128)(2,1)S(1)}, u32[]{:S(2)}, u32[]{:S(2)}) collective-permute-start(bf16[64,256]{1,0:T(8,128)(2,1)S(1)} %get-tuple-element.38), channel_id=1, source_target_pairs={{0,1},{1,0},{2,3},{3,2},{4,5},{5,4},{6,7},{7,6},{8,9},{9,8},{10,11... | collective-permute-start | bytes 98312 | tf_op jit(solution)/shard_map/ppermute | solution.py:32
  122.8 15.1 %collective-permute-done.3 = bf16[64,256]{1,0:T(8,128)(2,1)S(1)} collective-permute-done((bf16[64,256]{1,0:T(8,128)(2,1)S(1)}, bf16[64,256]{1,0:T(8,128)(2,1)S(1)}, u32[]{:S(2)}, u32[]{:S(2)}) %collective-permute-start.3) | collective-permute-done | bytes 32800 | tf_op jit(solution)/shard_map/ppermute | solution.py:32
  138.0 5.2 %collective-permute-start.4 = (bf16[128,256]{1,0:T(8,128)(2,1)S(1)}, bf16[128,256]{1,0:T(8,128)(2,1)S(1)}, u32[]{:S(2)}, u32[]{:S(2)}) collective-permute-start(bf16[128,256]{1,0:T(8,128)(2,1)S(1)} %maximum_select_fusion), channel_id=1, source_target_pairs={{0,0},{1,1},{2,128},{3,129},{4,256},{5,257},{6,384},{7,385},{64,64... | collective-permute-start | bytes 196616 | tf_op jit(solution)/shard_map/ppermute | solution.py:128
  143.2 6.1 %collective-permute-done.4 = bf16[128,256]{1,0:T(8,128)(2,1)S(1)} collective-permute-done((bf16[128,256]{1,0:T(8,128)(2,1)S(1)}, bf16[128,256]{1,0:T(8,128)(2,1)S(1)}, u32[]{:S(2)}, u32[]{:S(2)}) %collective-permute-start.4) | collective-permute-done | bytes 65568 | tf_op jit(solution)/shard_map/ppermute | solution.py:128
  149.3 2.5 %collective-permute-start.10 = (bf16[256,1024]{1,0:T(8,128)(2,1)S(1)}, bf16[256,1024]{1,0:T(8,128)(2,1)S(1)}, u32[]{:S(2)}, u32[]{:S(2)}) collective-permute-start(bf16[256,1024]{1,0:T(8,128)(2,1)S(1)} %bitcast.18), channel_id=1, source_target_pairs={{0,1},{1,0},{2,3},{3,2},{4,5},{5,4},{6,7},{7,6},{8,9},{9,8},{10,11... | collective-permute-start | bytes 1572872 | tf_op jit(solution)/shard_map/ppermute | solution.py:32
  151.8 5.2 %collective-permute-start.8 = (bf16[256,512]{1,0:T(8,128)(2,1)S(1)}, bf16[256,512]{1,0:T(8,128)(2,1)S(1)}, u32[]{:S(2)}, u32[]{:S(2)}) collective-permute-start(bf16[256,512]{1,0:T(8,128)(2,1)S(1)} %slice.71), channel_id=1, source_target_pairs={{0,64},{64,0},{1,65},{65,1},{2,66},{66,2},{3,67},{67,3},{4,68},{68... | collective-permute-start | bytes 786440 | tf_op jit(solution)/shard_map/ppermute | solution.py:28
  157.4 1.9 %collective-permute-start.11 = (bf16[256,1024]{1,0:T(8,128)(2,1)S(1)}, bf16[256,1024]{1,0:T(8,128)(2,1)S(1)}, u32[]{:S(2)}, u32[]{:S(2)}) collective-permute-start(bf16[256,1024]{1,0:T(8,128)(2,1)S(1)} %collective-permute-done.9), channel_id=1, source_target_pairs={{0,64},{64,0},{1,65},{65,1},{2,66},{66,2},{3,67},{67,3},{4,68},{68... | collective-permute-start | bytes 1572872 | tf_op jit(solution)/shard_map/ppermute | solution.py:28
  159.8 2.3 %collective-permute-done.10 = bf16[256,1024]{1,0:T(8,128)(2,1)S(1)} collective-permute-done((bf16[256,1024]{1,0:T(8,128)(2,1)S(1)}, bf16[256,1024]{1,0:T(8,128)(2,1)S(1)}, u32[]{:S(2)}, u32[]{:S(2)}) %collective-permute-start.10) | collective-permute-done | bytes 524320 | tf_op jit(solution)/shard_map/ppermute | solution.py:32
  162.1 5.3 %collective-permute-start.12 = (bf16[256,512]{1,0:T(8,128)(2,1)S(1)}, bf16[256,512]{1,0:T(8,128)(2,1)S(1)}, u32[]{:S(2)}, u32[]{:S(2)}) collective-permute-start(bf16[256,512]{1,0:T(8,128)(2,1)S(1)} %slice.89), channel_id=1, source_target_pairs={{0,64},{64,0},{1,65},{65,1},{2,66},{66,2},{3,67},{67,3},{4,68},{68... | collective-permute-start | bytes 786440 | tf_op jit(solution)/shard_map/ppermute | solution.py:28
  169.1 1.0 fusion.9
  (38 shorter events, 4.4 us)
Async XLA Ops:
  0.6 3.1 %copy-start.5 = (bf16[1024,256]{1,0:T(8,128)(2,1)S(1)}, bf16[1024,256]{1,0:T(8,128)(2,1)}, u32[]{:S(2)}) copy-start(bf16[1024,256]{1,0:T(8,128)(2,1)} %param.6) | copy-start | bytes 1572868
  3.8 25.9 %collective-permute-start = (bf16[1024,512]{1,0:T(8,128)(2,1)S(1)}, bf16[1024,512]{1,0:T(8,128)(2,1)S(1)}, u32[]{:S(2)}, u32[]{:S(2)}) collective-permute-start(bf16[1024,512]{1,0:T(8,128)(2,1)S(1)} %constant_dynamic-update-slice_fusion.own), channel_id=1, source_target_pairs={{0,1},{1,0},{2,3},{3,2},{4,5},{5,4},{6,7},{7,6},{8,9},{9,8},{10,11... | collective-permute-start | bytes 3145736 | tf_op jit(solution)/shard_map/ppermute | solution.py:32
  6.8 45.1 %all-to-all-start = ((bf16[64,64,128]{2,1,0:T(8,128)(2,1)}), bf16[64,64,128]{2,1,0:T(8,128)(2,1)S(1)}, u32[]{:S(2)}, u32[]{:S(2)}) async-start(bf16[64,64,128]{2,1,0:T(8,128)(2,1)} %bitcast.23), calls=%async_computation | async-start | bytes 2097152 | tf_op jit(solution)/shard_map/all_to_all | solution.py:84
  21.1 13.3 %collective-permute-start.1 = (bf16[1024,512]{1,0:T(8,128)(2,1)S(1)}, bf16[1024,512]{1,0:T(8,128)(2,1)}, u32[]{:S(2)}, u32[]{:S(2)}) collective-permute-start(bf16[1024,512]{1,0:T(8,128)(2,1)S(1)} %constant_dynamic-update-slice_fusion.own), channel_id=1, source_target_pairs={{0,64},{64,0},{1,65},{65,1},{2,66},{66,2},{3,67},{67,3},{4,68},{68... | collective-permute-start | bytes 3145736 | tf_op jit(solution)/shard_map/ppermute | solution.py:28
  29.7 22.2 %collective-permute-start.2 = (bf16[1024,512]{1,0:T(8,128)(2,1)S(1)}, bf16[1024,512]{1,0:T(8,128)(2,1)}, u32[]{:S(2)}, u32[]{:S(2)}) collective-permute-start(bf16[1024,512]{1,0:T(8,128)(2,1)S(1)} %collective-permute-done.own_pair), channel_id=1, source_target_pairs={{0,64},{64,0},{1,65},{65,1},{2,66},{66,2},{3,67},{67,3},{4,68},{68... | collective-permute-start | bytes 3145736 | tf_op jit(solution)/shard_map/ppermute | solution.py:28
  51.9 11.9 %copy-start.6 = (bf16[128,256]{1,0:T(8,128)(2,1)S(1)}, bf16[128,256]{1,0:T(8,128)(2,1)}, u32[]{:S(2)}) copy-start(bf16[128,256]{1,0:T(8,128)(2,1)} %param.7) | copy-start | bytes 196612
  54.8 0.8 copy-start.1
  55.6 0.8 copy-start.3
  56.4 0.8 copy-start
  57.2 22.4 %all-to-all-start.1 = ((bf16[4,64,1024]{2,1,0:T(8,128)(2,1)}), bf16[4,64,1024]{2,1,0:T(8,128)(2,1)S(1)}, u32[]{:S(2)}, u32[]{:S(2)}) async-start(bf16[4,64,1024]{2,1,0:T(8,128)(2,1)} %bitcast.21), calls=%async_computation.1 | async-start | bytes 1048576 | tf_op jit(solution)/shard_map/all_to_all | solution.py:104
  63.9 13.8 %collective-permute-start.5 = (bf16[128,256]{1,0:T(8,128)(2,1)S(1)}, bf16[128,256]{1,0:T(8,128)(2,1)S(1)}, u32[]{:S(2)}, u32[]{:S(2)}) collective-permute-start(bf16[128,256]{1,0:T(8,128)(2,1)S(1)} %copy-done.6), channel_id=1, source_target_pairs={{0,0},{1,1},{128,2},{129,3},{256,4},{257,5},{384,6},{385,7},{64,64... | collective-permute-start | bytes 196616 | tf_op jit(solution)/shard_map/ppermute | solution.py:90
  77.6 4.7 %collective-permute-start.6 = (bf16[64,256]{1,0:T(8,128)(2,1)S(1)}, bf16[64,256]{1,0:T(8,128)(2,1)S(1)}, u32[]{:S(2)}, u32[]{:S(2)}) collective-permute-start(bf16[64,256]{1,0:T(8,128)(2,1)S(1)} %get-tuple-element.35), channel_id=1, source_target_pairs={{0,1},{1,0},{2,3},{3,2},{4,5},{5,4},{6,7},{7,6},{8,9},{9,8},{10,11... | collective-permute-start | bytes 98312 | tf_op jit(solution)/shard_map/ppermute | solution.py:32
  100.7 13.5 %copy-start.2 = (bf16[256,1024]{1,0:T(8,128)(2,1)S(1)}, bf16[256,1024]{1,0:T(8,128)(2,1)}, u32[]{:S(2)}) copy-start(bf16[256,1024]{1,0:T(8,128)(2,1)} %copy-done.1) | copy-start | bytes 1572868
  100.7 16.8 %copy-start.4 = (bf16[256,1024]{1,0:T(8,128)(2,1)S(1)}, bf16[256,1024]{1,0:T(8,128)(2,1)}, u32[]{:S(2)}) copy-start(bf16[256,1024]{1,0:T(8,128)(2,1)} %copy-done.3) | copy-start | bytes 1572868
  100.7 69.4 %all-to-all-start.3 = ((bf16[64,64,128]{2,1,0:T(8,128)(2,1)}), bf16[64,64,128]{2,1,0:T(8,128)(2,1)S(1)}, u32[]{:S(2)}, u32[]{:S(2)}) async-start(bf16[64,64,128]{2,1,0:T(8,128)(2,1)} %bitcast.6), calls=%async_computation.3 | async-start | bytes 2097152 | tf_op jit(solution)/shard_map/all_to_all | solution.py:121
  114.3 45.1 %collective-permute-start.7 = (bf16[256,1024]{1,0:T(8,128)(2,1)S(1)}, bf16[256,1024]{1,0:T(8,128)(2,1)S(1)}, u32[]{:S(2)}, u32[]{:S(2)}) collective-permute-start(bf16[256,1024]{1,0:T(8,128)(2,1)S(1)} %copy-done.2), channel_id=1, source_target_pairs={{0,64},{64,0},{1,65},{65,1},{2,66},{66,2},{3,67},{67,3},{4,68},{68... | collective-permute-start | bytes 1572872 | tf_op jit(solution)/shard_map/ppermute | solution.py:28
  117.5 39.9 %collective-permute-start.9 = (bf16[256,1024]{1,0:T(8,128)(2,1)S(1)}, bf16[256,1024]{1,0:T(8,128)(2,1)S(1)}, u32[]{:S(2)}, u32[]{:S(2)}) collective-permute-start(bf16[256,1024]{1,0:T(8,128)(2,1)S(1)} %copy-done.4), channel_id=1, source_target_pairs={{0,1},{1,0},{2,3},{3,2},{4,5},{5,4},{6,7},{7,6},{8,9},{9,8},{10,11... | collective-permute-start | bytes 1572872 | tf_op jit(solution)/shard_map/ppermute | solution.py:32
  119.6 18.3 %collective-permute-start.3 = (bf16[64,256]{1,0:T(8,128)(2,1)S(1)}, bf16[64,256]{1,0:T(8,128)(2,1)S(1)}, u32[]{:S(2)}, u32[]{:S(2)}) collective-permute-start(bf16[64,256]{1,0:T(8,128)(2,1)S(1)} %get-tuple-element.38), channel_id=1, source_target_pairs={{0,1},{1,0},{2,3},{3,2},{4,5},{5,4},{6,7},{7,6},{8,9},{9,8},{10,11... | collective-permute-start | bytes 98312 | tf_op jit(solution)/shard_map/ppermute | solution.py:32
  138.0 11.3 %collective-permute-start.4 = (bf16[128,256]{1,0:T(8,128)(2,1)S(1)}, bf16[128,256]{1,0:T(8,128)(2,1)S(1)}, u32[]{:S(2)}, u32[]{:S(2)}) collective-permute-start(bf16[128,256]{1,0:T(8,128)(2,1)S(1)} %maximum_select_fusion), channel_id=1, source_target_pairs={{0,0},{1,1},{2,128},{3,129},{4,256},{5,257},{6,384},{7,385},{64,64... | collective-permute-start | bytes 196616 | tf_op jit(solution)/shard_map/ppermute | solution.py:128
  149.3 12.9 %collective-permute-start.10 = (bf16[256,1024]{1,0:T(8,128)(2,1)S(1)}, bf16[256,1024]{1,0:T(8,128)(2,1)S(1)}, u32[]{:S(2)}, u32[]{:S(2)}) collective-permute-start(bf16[256,1024]{1,0:T(8,128)(2,1)S(1)} %bitcast.18), channel_id=1, source_target_pairs={{0,1},{1,0},{2,3},{3,2},{4,5},{5,4},{6,7},{7,6},{8,9},{9,8},{10,11... | collective-permute-start | bytes 1572872 | tf_op jit(solution)/shard_map/ppermute | solution.py:32
  151.8 7.6 %collective-permute-start.8 = (bf16[256,512]{1,0:T(8,128)(2,1)S(1)}, bf16[256,512]{1,0:T(8,128)(2,1)S(1)}, u32[]{:S(2)}, u32[]{:S(2)}) collective-permute-start(bf16[256,512]{1,0:T(8,128)(2,1)S(1)} %slice.71), channel_id=1, source_target_pairs={{0,64},{64,0},{1,65},{65,1},{2,66},{66,2},{3,67},{67,3},{4,68},{68... | collective-permute-start | bytes 786440 | tf_op jit(solution)/shard_map/ppermute | solution.py:28
  157.4 11.1 %collective-permute-start.11 = (bf16[256,1024]{1,0:T(8,128)(2,1)S(1)}, bf16[256,1024]{1,0:T(8,128)(2,1)S(1)}, u32[]{:S(2)}, u32[]{:S(2)}) collective-permute-start(bf16[256,1024]{1,0:T(8,128)(2,1)S(1)} %collective-permute-done.9), channel_id=1, source_target_pairs={{0,64},{64,0},{1,65},{65,1},{2,66},{66,2},{3,67},{67,3},{4,68},{68... | collective-permute-start | bytes 1572872 | tf_op jit(solution)/shard_map/ppermute | solution.py:28
  162.1 6.4 %collective-permute-start.12 = (bf16[256,512]{1,0:T(8,128)(2,1)S(1)}, bf16[256,512]{1,0:T(8,128)(2,1)S(1)}, u32[]{:S(2)}, u32[]{:S(2)}) collective-permute-start(bf16[256,512]{1,0:T(8,128)(2,1)S(1)} %slice.89), channel_id=1, source_target_pairs={{0,64},{64,0},{1,65},{65,1},{2,66},{66,2},{3,67},{67,3},{4,68},{68... | collective-permute-start | bytes 786440 | tf_op jit(solution)/shard_map/ppermute | solution.py:28

commit v4 on v1

v4 whole, which is shorter than its diff:
```python
import jax
import jax.numpy as jnp
from jax import lax
from jax.experimental import pallas as pl
from jax.experimental.pallas import tpu as pltpu
from jax.sharding import Mesh, PartitionSpec as P

PLANE = ("x", "zl", "zh")
F32 = jnp.float32
BF16 = jnp.bfloat16
LAST = (((1,), (1,)), ((), ()))
ROWS = (((0,), (0,)), ((), ()))


def regroup():
    pairs = []
    for zl in range(4):
        for co in range(2):
            for c in range(2):
                for a in range(4):
                    work = (zl * 2 + co) * 8 + 4 * c + a
                    home = (a * 2 + co) * 8 + 2 * zl + (co ^ c)
                    pairs.append((work, home))
    return pairs


def swap_cores(value):
    return lax.ppermute(value, "co", [(0, 1), (1, 0)])


def spread(value, axes, count):
    return lax.all_to_all(jnp.tile(value, (count, 1)), axes, 0, 0, tiled=True)


def forward_kernel(tiles, own_gate, own_up, other_gate, other_up, parts, rows):
    for x in range(4):
        for zl in range(4):
            for zh in range(2):
                column = 128 * (2 * x + zh)
                rows[128 * zl : 128 * zl + 128, column : column + 128] = tiles[x, zl, zh]
    for at, weight in enumerate((own_gate, own_up, other_gate, other_up)):
        sums = jnp.dot(rows[...], weight[...], preferred_element_type=F32)
        row, column = 512 * (at // 2), 256 * (at % 2)
        parts[row : row + 512, column : column + 256] = sums.astype(BF16)


def backward_kernel(grads, own_gate, own_up, other_gate, other_up, blocks):
    for x in range(4):
        rows = slice(256 * x, 256 * x + 256)
        sums = 0.0
        for at, weight in enumerate((own_gate, own_up, other_gate, other_up)):
            row, column = 512 * (at // 2), 256 * (at % 2)
            sums += lax.dot_general(
                grads[row : row + 512, column : column + 256],
                weight[rows],
                LAST,
                preferred_element_type=F32,
            )
        sums = sums.astype(BF16)
        for zl in range(4):
            for zh in range(2):
                blocks[x, zl, zh] = sums[128 * zl : 128 * zl + 128, 128 * zh : 128 * zh + 128]


def call(kernel, outputs, inputs):
    vmem = pl.BlockSpec(memory_space=pltpu.VMEM)
    return pl.pallas_call(
        kernel,
        out_shape=[jax.ShapeDtypeStruct(shape, BF16) for shape in outputs],
        in_specs=[vmem] * len(inputs),
        out_specs=[vmem] * len(outputs),
        compiler_params=pltpu.CompilerParams(vmem_limit_bytes=40 * 1024 * 1024),
    )(*inputs)


def gather_rows(tokens):
    return spread(tokens, PLANE, 32)


def body(tokens, gate_weight, up_weight, hidden_grad):
    to_home = regroup()
    to_work = [(home, work) for work, home in to_home]
    tiles = gather_rows(tokens)
    weights = (gate_weight, up_weight, swap_cores(gate_weight), swap_cores(up_weight))
    upstream = lax.ppermute(hidden_grad, ("zl", "co", "y"), to_work)
    parts, rows = call(
        forward_kernel,
        [(1024, 512), (512, 1024)],
        (tiles.reshape(4, 4, 2, 128, 128),) + weights,
    )
    parts = lax.all_to_all(parts, "y", 0, 0, tiled=True)
    sums = jnp.sum(parts.reshape(8, 128, 512).astype(F32), axis=0)
    gate_sum, up_sum = sums[:, :256], sums[:, 256:]
    sigmoid_gate = jax.nn.sigmoid(gate_sum)
    activated = gate_sum * sigmoid_gate
    hidden = (activated * up_sum).astype(BF16)
    upstream = upstream.astype(F32)
    gate_grad = upstream * up_sum * sigmoid_gate * (1.0 + gate_sum * (1.0 - sigmoid_gate))
    up_grad = upstream * activated
    mine = jnp.concatenate([gate_grad.astype(BF16), up_grad.astype(BF16)], axis=1)
    grads = spread(mine, "y", 8)
    (blocks,) = call(backward_kernel, [(4, 4, 2, 128, 128)], (grads,) + weights)
    blocks, grads, rows = lax.optimization_barrier((blocks, grads, rows))
    blocks = lax.all_to_all(blocks.reshape(32 * 128, 128), PLANE, 0, 0, tiled=True)
    received_grads = swap_cores(grads[512:])
    other_rows = swap_cores(rows)
    hidden = lax.ppermute(hidden, ("zl", "co", "y"), to_home)
    wgrad = lax.dot_general(rows, grads[:512], ROWS, preferred_element_type=F32)
    wgrad += lax.dot_general(other_rows, received_grads, ROWS, preferred_element_type=F32)
    wgrad = wgrad.astype(BF16)
    input_grad = jnp.sum(blocks.reshape(32, 128, 128).astype(F32), axis=0).astype(BF16)
    return hidden, input_grad, wgrad[:, :256], wgrad[:, 256:]


def solution(mesh):
    fine = Mesh(mesh.devices.reshape(4, 2, 4, 2, 8), ("zl", "co", "x", "zh", "y"))
    gx, gy, gz = ("zl", "co"), ("x", "zh"), ("y",)
    in_specs = (P(gx, gz + gy), P(gz, gy + gx), P(gz, gy + gx), P(gx, gy + gz))
    out_specs = (P(gx, gy + gz), P(gx, gz + gy), P(gz, gy + gx), P(gz, gy + gx))
    return jax.shard_map(body, mesh=fine, in_specs=in_specs, out_specs=out_specs, check_vma=False)
```

time: 162 us -> 155 us (0.957)
  matrix products: 6.81 us -> 1.49 us
  waiting for transfers between devices: 73.8 us -> 69.7 us
  Pallas kernels: 0 us -> 3.53 us
  starting transfers between devices: 37.3 us -> 40.3 us
  local copies, waits for them, and re-layouts: 7.45 us -> 5.82 us
    dot_general x6 -> x2, matrix products: 6.81 us -> 1.49 us  [the longest x1 0.75 us: body(): wgrad = lax.dot_general(rows, grads[:512], ROWS, preferred_element_type=F32)]
    all_to_all x1, waiting for transfers between devices: 25.7 us -> 21.8 us  [spread(): return lax.all_to_all(jnp.tile(value, (count, 1)), axes, 0, 0, tiled=True)]
    all_to_all x1, waiting for transfers between devices: 24.1 us -> 20.5 us  [body(): lax.all_to_all(blocks.reshape(32 * 128, 128), PLANE, 0, 0, tiled=True)]
    pallas_call x0 -> x2, Pallas kernels: none -> 3.53 us  [call(): pl.pallas_call(kernel, out_shape=[jax.ShapeDtypeStruct(shape, BF16) for s...]
    ppermute x3 -> x4, starting transfers between devices: 6.25 us -> 8.65 us  [swap_cores(): return lax.ppermute(value, 'co', [(0, 1), (1, 0)])]
    ppermute x3 -> x4, waiting for transfers between devices: 0.09 us -> 2.34 us  [swap_cores(): return lax.ppermute(value, 'co', [(0, 1), (1, 0)])]
  transfers between devices with their start and end apart: 8 -> 9, of which waited for: 4 -> 5; matrix products, arithmetic and copies ran while one was open for 3% -> 2% of each run, Pallas kernels for 0% -> 0%
where the time goes in v4:
time: 155 us
  waiting for transfers between devices  69.7 us (45%)
  starting transfers between devices  40.3 us (26%)
  blocking collectives  32 us (21%)
  local copies, waits for them, and re-layouts  5.82 us (4%)
  Pallas kernels  3.53 us (2%)
    all_to_all x1, blocking collectives, spread(): return lax.all_to_all(jnp.tile(value, (count, 1)), axes, 0, 0, tiled=True)  32 us
    all_to_all x1, waiting for transfers between devices, body(): parts = lax.all_to_all(parts, 'y', 0, 0, tiled=True)  25.1 us
    all_to_all x1, waiting for transfers between devices, spread(): return lax.all_to_all(jnp.tile(value, (count, 1)), axes, 0, 0, tiled=True)  21.8 us
    all_to_all x1, waiting for transfers between devices, body(): lax.all_to_all(blocks.reshape(32 * 128, 128), PLANE, 0, 0, tiled=True)  20.5 us
    all_to_all x1, starting transfers between devices, spread(): return lax.all_to_all(jnp.tile(value, (count, 1)), axes, 0, 0, tiled=True)  13.5 us
    all_to_all x1, starting transfers between devices, body(): lax.all_to_all(blocks.reshape(32 * 128, 128), PLANE, 0, 0, tiled=True)  9.79 us
    ppermute x4, starting transfers between devices, swap_cores(): return lax.ppermute(value, 'co', [(0, 1), (1, 0)])  8.65 us
    all_to_all x1, starting transfers between devices, body(): parts = lax.all_to_all(parts, 'y', 0, 0, tiled=True)  7.1 us
  transfers between devices with their start and end apart: 9, of which 5 were waited for; matrix products, arithmetic and copies ran while one was open for 2% of the time, Pallas kernels for 0%

profile of v4, /device:TPU:6, one launch (start us, length us, event | category | flops | bytes accessed | tf_op | source)
XLA Modules:
  0.0 154.7 jit_solution(11213832760102273360)
XLA Ops:
  0.7 2.1 %tile.4 = bf16[32,128,128]{2,1,0:T(8,128)(2,1)} broadcast(bf16[128,128]{1,0:T(8,128)(2,1)} %param.4), dimensions={1,2} | broadcast | bytes 1081344 | tf_op jit(solution)/shard_map/tile | solution.py:32
  2.7 13.5 %all-to-all-start = ((bf16[32,128,128]{2,1,0:T(8,128)(2,1)}), bf16[32,128,128]{2,1,0:T(8,128)(2,1)S(1)}, u32[]{:S(2)}, u32[]{:S(2)}) async-start(bf16[32,128,128]{2,1,0:T(8,128)(2,1)} %tile.4), calls=%async_computation | async-start | bytes 2097152 | tf_op jit(solution)/shard_map/all_to_all | solution.py:32
  16.2 1.9 %collective-permute-start = (bf16[1024,256]{1,0:T(8,128)(2,1)S(1)}, bf16[1024,256]{1,0:T(8,128)(2,1)S(1)}, u32[]{:S(2)}, u32[]{:S(2)}) collective-permute-start(bf16[1024,256]{1,0:T(8,128)(2,1)S(1)} %copy-done), channel_id=1, source_target_pairs={{0,64},{64,0},{1,65},{65,1},{2,66},{66,2},{3,67},{67,3},{4,68},{68... | collective-permute-start | bytes 1572872 | tf_op jit(solution)/shard_map/ppermute | solution.py:28
  18.1 2.4 %collective-permute-start.1 = (bf16[1024,256]{1,0:T(8,128)(2,1)S(1)}, bf16[1024,256]{1,0:T(8,128)(2,1)S(1)}, u32[]{:S(2)}, u32[]{:S(2)}) collective-permute-start(bf16[1024,256]{1,0:T(8,128)(2,1)S(1)} %copy-done.1), channel_id=1, source_target_pairs={{0,64},{64,0},{1,65},{65,1},{2,66},{66,2},{3,67},{67,3},{4,68},{68... | collective-permute-start | bytes 1572872 | tf_op jit(solution)/shard_map/ppermute | solution.py:28
  20.5 0.0 collective-permute-done.other_gate
  20.5 1.5 collective-permute-done.1.other_up
  22.0 21.8 %all-to-all-done = bf16[32,128,128]{2,1,0:T(8,128)(2,1)S(1)} async-done(((bf16[32,128,128]{2,1,0:T(8,128)(2,1)}), bf16[32,128,128]{2,1,0:T(8,128)(2,1)S(1)}, u32[]{:S(2)}, u32[]{:S(2)}) %all-to-all-start) | async-done | bytes 1048608 | tf_op jit(solution)/shard_map/all_to_all | solution.py:32
  43.9 1.3 shard_map.75
  45.2 1.0 copy-done.2
  46.2 1.0 copy-done.3
  47.1 7.1 %all-to-all-start.1 = ((bf16[8,128,512]{2,1,0:T(8,128)(2,1)}), bf16[8,128,512]{2,1,0:T(8,128)(2,1)S(1)}, u32[]{:S(2)}, u32[]{:S(2)}) async-start(bf16[8,128,512]{2,1,0:T(8,128)(2,1)} %bitcast.11), calls=%async_computation.1 | async-start | bytes 2097152 | tf_op jit(solution)/shard_map/all_to_all | solution.py:91
  54.2 0.7 collective-permute-start.3
  54.9 25.1 %all-to-all-done.1 = bf16[8,128,512]{2,1,0:T(8,128)(2,1)S(1)} async-done(((bf16[8,128,512]{2,1,0:T(8,128)(2,1)}), bf16[8,128,512]{2,1,0:T(8,128)(2,1)S(1)}, u32[]{:S(2)}, u32[]{:S(2)}) %all-to-all-start.1) | async-done | bytes 1048608 | tf_op jit(solution)/shard_map/all_to_all | solution.py:91
  80.0 0.1 convert_reduce_fusion
  80.1 0.0 collective-permute-done.3
  80.1 0.1 fusion.3
  80.3 0.1 tile.5
  80.3 32.0 %all_to_all.32 = bf16[8,128,512]{2,1,0:T(8,128)(2,1)S(1)} all-to-all(bf16[8,128,512]{2,1,0:T(8,128)(2,1)S(1)} %tile.5), channel_id=1, replica_groups=mesh['zl'=4,'co'=2,'x'=4,'zh'=2,'y'=8] {'y'}, dimensions={0} | all-to-all | bytes 2097152 | tf_op jit(solution)/shard_map/all_to_all | solution.py:32
  112.3 2.3 %shard_map.76 = bf16[4,4,2,128,128]{4,3,2,1,0:T(8,128)(2,1)} custom-call(bf16[1024,512]{1,0:T(8,128)(2,1)S(1)} %bitcast.7, bf16[1024,256]{1,0:T(8,128)(2,1)S(1)} %copy-done, bf16[1024,256]{1,0:T(8,128)(2,1)S(1)} %copy-done.1, bf16[1024,256]{1,0:T(8,128)(2,1)S(1)} %collective-permute-done.other_gate, bf16[1024,256]{1,0:T(8,128)(2,1)S(1)} %collective-permute-done.1.other_up), custom_call_target="tpu_custom_call" | custom-call | tf_op jit(solution)/shard_map/pallas_call | solution.py:67
  114.6 9.8 %all-to-all-start.3 = ((bf16[32,128,128]{2,1,0:T(8,128)(2,1)}), bf16[32,128,128]{2,1,0:T(8,128)(2,1)S(1)}, u32[]{:S(2)}, u32[]{:S(2)}) async-start(bf16[32,128,128]{2,1,0:T(8,128)(2,1)} %bitcast.3), calls=%async_computation.3 | async-start | bytes 2097152 | tf_op jit(solution)/shard_map/all_to_all | solution.py:104
  124.4 1.9 %collective-permute-start.4 = (bf16[512,1024]{1,0:T(8,128)(2,1)S(1)}, bf16[512,1024]{1,0:T(8,128)(2,1)S(1)}, u32[]{:S(2)}, u32[]{:S(2)}) collective-permute-start(bf16[512,1024]{1,0:T(8,128)(2,1)S(1)} %copy-done.4), channel_id=1, source_target_pairs={{0,64},{64,0},{1,65},{65,1},{2,66},{66,2},{3,67},{67,3},{4,68},{68... | collective-permute-start | bytes 3145736 | tf_op jit(solution)/shard_map/ppermute | solution.py:28
  126.4 2.4 %collective-permute-start.5 = (bf16[512,512]{1,0:T(8,128)(2,1)S(1)}, bf16[512,512]{1,0:T(8,128)(2,1)S(1)}, u32[]{:S(2)}, u32[]{:S(2)}) collective-permute-start(bf16[512,512]{1,0:T(8,128)(2,1)S(1)} %slice.21), channel_id=1, source_target_pairs={{0,64},{64,0},{1,65},{65,1},{2,66},{66,2},{3,67},{67,3},{4,68},{68... | collective-permute-start | bytes 1572872 | tf_op jit(solution)/shard_map/ppermute | solution.py:28
  128.8 0.7 collective-permute-start.2
  129.5 0.0 collective-permute-done.2
  129.5 0.8 collective-permute-done.5
  130.3 0.0 collective-permute-done.4
  130.3 0.7 fusion.7
  131.1 0.7 add_convert_fusion
  131.8 1.0 fusion.6
  132.8 20.5 %all-to-all-done.3 = bf16[32,128,128]{2,1,0:T(8,128)(2,1)S(1)} async-done(((bf16[32,128,128]{2,1,0:T(8,128)(2,1)}), bf16[32,128,128]{2,1,0:T(8,128)(2,1)S(1)}, u32[]{:S(2)}, u32[]{:S(2)}) %all-to-all-start.3) | async-done | bytes 1048608 | tf_op jit(solution)/shard_map/all_to_all | solution.py:104
  153.3 0.8 reduce_sum.22
  154.1 0.6 copy.9
  (12 shorter events, 0.1 us)
Async XLA Ops:
  0.6 15.5 %copy-start = (bf16[1024,256]{1,0:T(8,128)(2,1)S(1)}, bf16[1024,256]{1,0:T(8,128)(2,1)}, u32[]{:S(2)}) copy-start(bf16[1024,256]{1,0:T(8,128)(2,1)} %own_gate.3) | copy-start | bytes 1572868
  0.6 17.5 %copy-start.1 = (bf16[1024,256]{1,0:T(8,128)(2,1)S(1)}, bf16[1024,256]{1,0:T(8,128)(2,1)}, u32[]{:S(2)}) copy-start(bf16[1024,256]{1,0:T(8,128)(2,1)} %own_up.3) | copy-start | bytes 1572868
  2.7 41.2 %all-to-all-start = ((bf16[32,128,128]{2,1,0:T(8,128)(2,1)}), bf16[32,128,128]{2,1,0:T(8,128)(2,1)S(1)}, u32[]{:S(2)}, u32[]{:S(2)}) async-start(bf16[32,128,128]{2,1,0:T(8,128)(2,1)} %tile.4), calls=%async_computation | async-start | bytes 2097152 | tf_op jit(solution)/shard_map/all_to_all | solution.py:32
  16.2 4.4 %collective-permute-start = (bf16[1024,256]{1,0:T(8,128)(2,1)S(1)}, bf16[1024,256]{1,0:T(8,128)(2,1)S(1)}, u32[]{:S(2)}, u32[]{:S(2)}) collective-permute-start(bf16[1024,256]{1,0:T(8,128)(2,1)S(1)} %copy-done), channel_id=1, source_target_pairs={{0,64},{64,0},{1,65},{65,1},{2,66},{66,2},{3,67},{67,3},{4,68},{68... | collective-permute-start | bytes 1572872 | tf_op jit(solution)/shard_map/ppermute | solution.py:28
  18.1 3.9 %collective-permute-start.1 = (bf16[1024,256]{1,0:T(8,128)(2,1)S(1)}, bf16[1024,256]{1,0:T(8,128)(2,1)S(1)}, u32[]{:S(2)}, u32[]{:S(2)}) collective-permute-start(bf16[1024,256]{1,0:T(8,128)(2,1)S(1)} %copy-done.1), channel_id=1, source_target_pairs={{0,64},{64,0},{1,65},{65,1},{2,66},{66,2},{3,67},{67,3},{4,68},{68... | collective-permute-start | bytes 1572872 | tf_op jit(solution)/shard_map/ppermute | solution.py:28
  43.9 10.3 %copy-start.5 = (bf16[128,256]{1,0:T(8,128)(2,1)S(1)}, bf16[128,256]{1,0:T(8,128)(2,1)}, u32[]{:S(2)}) copy-start(bf16[128,256]{1,0:T(8,128)(2,1)} %param.7) | copy-start | bytes 196612
  45.2 1.0 copy-start.2
  46.1 1.0 copy-start.3
  47.1 32.8 %all-to-all-start.1 = ((bf16[8,128,512]{2,1,0:T(8,128)(2,1)}), bf16[8,128,512]{2,1,0:T(8,128)(2,1)S(1)}, u32[]{:S(2)}, u32[]{:S(2)}) async-start(bf16[8,128,512]{2,1,0:T(8,128)(2,1)} %bitcast.11), calls=%async_computation.1 | async-start | bytes 2097152 | tf_op jit(solution)/shard_map/all_to_all | solution.py:91
  54.2 25.9 %collective-permute-start.3 = (bf16[128,256]{1,0:T(8,128)(2,1)S(1)}, bf16[128,256]{1,0:T(8,128)(2,1)S(1)}, u32[]{:S(2)}, u32[]{:S(2)}) collective-permute-start(bf16[128,256]{1,0:T(8,128)(2,1)S(1)} %copy-done.5), channel_id=1, source_target_pairs={{0,0},{128,1},{256,2},{384,3},{1,4},{129,5},{257,6},{385,7},{65,64... | collective-permute-start | bytes 196616 | tf_op jit(solution)/shard_map/ppermute | solution.py:85
  114.6 9.8 %copy-start.4 = (bf16[512,1024]{1,0:T(8,128)(2,1)S(1)}, bf16[512,1024]{1,0:T(8,128)(2,1)}, u32[]{:S(2)}) copy-start(bf16[512,1024]{1,0:T(8,128)(2,1)} %copy-done.3) | copy-start | bytes 3145732
  114.6 38.7 %all-to-all-start.3 = ((bf16[32,128,128]{2,1,0:T(8,128)(2,1)}), bf16[32,128,128]{2,1,0:T(8,128)(2,1)S(1)}, u32[]{:S(2)}, u32[]{:S(2)}) async-start(bf16[32,128,128]{2,1,0:T(8,128)(2,1)} %bitcast.3), calls=%async_computation.3 | async-start | bytes 2097152 | tf_op jit(solution)/shard_map/all_to_all | solution.py:104
  124.4 5.9 %collective-permute-start.4 = (bf16[512,1024]{1,0:T(8,128)(2,1)S(1)}, bf16[512,1024]{1,0:T(8,128)(2,1)S(1)}, u32[]{:S(2)}, u32[]{:S(2)}) collective-permute-start(bf16[512,1024]{1,0:T(8,128)(2,1)S(1)} %copy-done.4), channel_id=1, source_target_pairs={{0,64},{64,0},{1,65},{65,1},{2,66},{66,2},{3,67},{67,3},{4,68},{68... | collective-permute-start | bytes 3145736 | tf_op jit(solution)/shard_map/ppermute | solution.py:28
  126.4 3.9 %collective-permute-start.5 = (bf16[512,512]{1,0:T(8,128)(2,1)S(1)}, bf16[512,512]{1,0:T(8,128)(2,1)S(1)}, u32[]{:S(2)}, u32[]{:S(2)}) collective-permute-start(bf16[512,512]{1,0:T(8,128)(2,1)S(1)} %slice.21), channel_id=1, source_target_pairs={{0,64},{64,0},{1,65},{65,1},{2,66},{66,2},{3,67},{67,3},{4,68},{68... | collective-permute-start | bytes 1572872 | tf_op jit(solution)/shard_map/ppermute | solution.py:28
  128.8 0.7 collective-permute-start.2

commit v5 on v4

--- a/solution.py
+++ b/solution.py
@@ -5,7 +5,7 @@
 from jax.experimental.pallas import tpu as pltpu
 from jax.sharding import Mesh, PartitionSpec as P
 
-PLANE = ("x", "zl", "zh")
+RING = ("zl", "zh")
 F32 = jnp.float32
 BF16 = jnp.bfloat16
 LAST = (((1,), (1,)), ((), ()))
@@ -74,7 +74,7 @@
 
 
 def gather_rows(tokens):
-    return spread(tokens, PLANE, 32)
+    return spread(spread(tokens, RING, 8), "x", 4)
 
 
 def body(tokens, gate_weight, up_weight, hidden_grad):
@@ -83,6 +83,7 @@
     tiles = gather_rows(tokens)
     weights = (gate_weight, up_weight, swap_cores(gate_weight), swap_cores(up_weight))
     upstream = lax.ppermute(hidden_grad, ("zl", "co", "y"), to_work)
+    tiles, upstream = lax.optimization_barrier((tiles, upstream))
     parts, rows = call(
         forward_kernel,
         [(1024, 512), (512, 1024)],
@@ -101,14 +102,16 @@
     grads = spread(mine, "y", 8)
     (blocks,) = call(backward_kernel, [(4, 4, 2, 128, 128)], (grads,) + weights)
     blocks, grads, rows = lax.optimization_barrier((blocks, grads, rows))
-    blocks = lax.all_to_all(blocks.reshape(32 * 128, 128), PLANE, 0, 0, tiled=True)
+    blocks = lax.all_to_all(blocks.reshape(32 * 128, 128), "x", 0, 0, tiled=True)
+    blocks = jnp.sum(blocks.reshape(4, 8 * 128, 128).astype(F32), axis=0).astype(BF16)
+    blocks = lax.all_to_all(blocks, RING, 0, 0, tiled=True)
     received_grads = swap_cores(grads[512:])
     other_rows = swap_cores(rows)
     hidden = lax.ppermute(hidden, ("zl", "co", "y"), to_home)
     wgrad = lax.dot_general(rows, grads[:512], ROWS, preferred_element_type=F32)
     wgrad += lax.dot_general(other_rows, received_grads, ROWS, preferred_element_type=F32)
     wgrad = wgrad.astype(BF16)
-    input_grad = jnp.sum(blocks.reshape(32, 128, 128).astype(F32), axis=0).astype(BF16)
+    input_grad = jnp.sum(blocks.reshape(8, 128, 128).astype(F32), axis=0).astype(BF16)
     return hidden, input_grad, wgrad[:, :256], wgrad[:, 256:]
 
 

time: 155 us -> 149 us (0.961); the launches traced: 155 us -> 146 us
  blocking collectives: 32 us -> 86.2 us
  waiting for transfers between devices: 69.7 us -> 20.3 us
  starting transfers between devices: 40.3 us -> 24.7 us
  matrix products: 1.49 us -> 3.75 us
    all_to_all x0 -> x1, blocking collectives: none -> 38.1 us  [body(): parts = lax.all_to_all(parts, 'y', 0, 0, tiled=True)]
    all_to_all x2, waiting for transfers between devices: 45.5 us -> 14.3 us  [the longest x1 10.3 us: body(): lax.all_to_all(blocks.reshape(32 * 128, 128), 'x', 0, 0, tiled=True)]
    all_to_all x1 -> x2, blocking collectives: 32 us -> 48.1 us  [spread(): return lax.all_to_all(jnp.tile(value, (count, 1)), axes, 0, 0, tiled=True)]
    all_to_all x1, waiting for transfers between devices: 21.8 us -> 6 us  [spread(): return lax.all_to_all(jnp.tile(value, (count, 1)), axes, 0, 0, tiled=True)]
    all_to_all x1, starting transfers between devices: 13.5 us -> 4.77 us  [spread(): return lax.all_to_all(jnp.tile(value, (count, 1)), axes, 0, 0, tiled=True)]
    all_to_all x2, starting transfers between devices: 16.9 us -> 10.5 us  [the longest x1 5.67 us: body(): blocks = lax.all_to_all(blocks, RING, 0, 0, tiled=True)]
    ppermute x4, waiting for transfers between devices: 2.34 us -> 0.01 us  [swap_cores(): return lax.ppermute(value, 'co', [(0, 1), (1, 0)])]
    unnamed x13 -> x7, local copies, waits for them, and re-layouts: 2.61 us -> 0.64 us
  transfers between devices with their start and end apart: 9 -> 9, of which waited for: 5 -> 3; matrix products, arithmetic and copies ran while one was open for 2% -> 4% of each run, Pallas kernels for 0% -> 0%
where the time goes in v5:
time: 149 us; the launch traced here: 146 us
  blocking collectives  86.2 us (58%)
  starting transfers between devices  24.7 us (17%)
  waiting for transfers between devices  20.3 us (14%)
  local copies, waits for them, and re-layouts  4.56 us (3%)
  Pallas kernels  3.77 us (3%)
  matrix products  3.75 us (3%)
  other arithmetic  1.81 us (1%)
    all_to_all x2, blocking collectives, spread(): return lax.all_to_all(jnp.tile(value, (count, 1)), axes, 0, 0, tiled=True)  48.1 us
    all_to_all x1, blocking collectives, body(): parts = lax.all_to_all(parts, 'y', 0, 0, tiled=True)  38.1 us
    all_to_all x1, waiting for transfers between devices, body(): lax.all_to_all(blocks.reshape(32 * 128, 128), 'x', 0, 0, tiled=True)  10.3 us
    ppermute x4, starting transfers between devices, swap_cores(): return lax.ppermute(value, 'co', [(0, 1), (1, 0)])  8.13 us
    all_to_all x1, waiting for transfers between devices, spread(): return lax.all_to_all(jnp.tile(value, (count, 1)), axes, 0, 0, tiled=True)  6 us
    all_to_all x1, starting transfers between devices, body(): blocks = lax.all_to_all(blocks, RING, 0, 0, tiled=True)  5.67 us
    all_to_all x1, starting transfers between devices, body(): lax.all_to_all(blocks.reshape(32 * 128, 128), 'x', 0, 0, tiled=True)  4.81 us
    all_to_all x1, starting transfers between devices, spread(): return lax.all_to_all(jnp.tile(value, (count, 1)), axes, 0, 0, tiled=True)  4.77 us
  transfers between devices with their start and end apart: 9, of which 3 were waited for; matrix products, arithmetic and copies ran while one was open for 4% of the time, Pallas kernels for 0%

profile of v5, /device:TPU:6, one launch (start us, length us, event | category | flops | bytes accessed | tf_op | source)
XLA Modules:
  0.0 145.9 jit_solution(5941799306746344357)
XLA Ops:
  0.7 0.9 tile.8
  1.5 19.0 %all_to_all.50 = bf16[8,128,128]{2,1,0:T(8,128)(2,1)S(1)} all-to-all(bf16[8,128,128]{2,1,0:T(8,128)(2,1)S(1)} %tile.8), channel_id=1, replica_groups=mesh['zl'=4,'co'=2,'x'=4,'zh'=2,'y'=8] {'zl','zh'}, dimensions={0} | all-to-all | bytes 524288 | tf_op jit(solution)/shard_map/all_to_all | solution.py:32
  20.5 1.1 tile.10
  21.6 4.8 %all-to-all-start.1 = ((bf16[4,1024,128]{2,1,0:T(8,128)(2,1)}), bf16[4,1024,128]{2,1,0:T(8,128)(2,1)S(1)}, u32[]{:S(2)}, u32[]{:S(2)}) async-start(bf16[4,1024,128]{2,1,0:T(8,128)(2,1)} %tile.10), calls=%async_computation.1 | async-start | bytes 2097152 | tf_op jit(solution)/shard_map/all_to_all | solution.py:32
  26.4 1.9 %collective-permute-start.1 = (bf16[1024,256]{1,0:T(8,128)(2,1)S(1)}, bf16[1024,256]{1,0:T(8,128)(2,1)S(1)}, u32[]{:S(2)}, u32[]{:S(2)}) collective-permute-start(bf16[1024,256]{1,0:T(8,128)(2,1)S(1)} %copy-done), channel_id=1, source_target_pairs={{0,64},{64,0},{1,65},{65,1},{2,66},{66,2},{3,67},{67,3},{4,68},{68... | collective-permute-start | bytes 1572872 | tf_op jit(solution)/shard_map/ppermute | solution.py:28
  28.3 2.4 %collective-permute-start.2 = (bf16[1024,256]{1,0:T(8,128)(2,1)S(1)}, bf16[1024,256]{1,0:T(8,128)(2,1)S(1)}, u32[]{:S(2)}, u32[]{:S(2)}) collective-permute-start(bf16[1024,256]{1,0:T(8,128)(2,1)S(1)} %copy-done.1), channel_id=1, source_target_pairs={{0,64},{64,0},{1,65},{65,1},{2,66},{66,2},{3,67},{67,3},{4,68},{68... | collective-permute-start | bytes 1572872 | tf_op jit(solution)/shard_map/ppermute | solution.py:28
  30.7 0.7 collective-permute-start
  31.4 0.0 collective-permute-done
  31.4 6.0 %all-to-all-done.1 = bf16[4,1024,128]{2,1,0:T(8,128)(2,1)S(1)} async-done(((bf16[4,1024,128]{2,1,0:T(8,128)(2,1)}), bf16[4,1024,128]{2,1,0:T(8,128)(2,1)S(1)}, u32[]{:S(2)}, u32[]{:S(2)}) %all-to-all-start.1) | async-done | bytes 1048608 | tf_op jit(solution)/shard_map/all_to_all | solution.py:32
  37.4 1.5 %shard_map.75 = (bf16[1024,512]{1,0:T(8,128)(2,1)S(1)}, bf16[512,1024]{1,0:T(8,128)(2,1)}) custom-call(bf16[4,4,2,128,128]{4,3,2,1,0:T(8,128)(2,1)S(1)} %bitcast.13, bf16[1024,256]{1,0:T(8,128)(2,1)S(1)} %copy-done, bf16[1024,256]{1,0:T(8,128)(2,1)S(1)} %copy-done.1, bf16[1024,256]{1,0:T(8,128)(2,1)S(1)} %collective-permute-done.1.other_gate, ...), custom_call_target="tpu_custom_call" | custom-call | tf_op jit(solution)/shard_map/pallas_call | solution.py:67
  38.9 38.1 %all_to_all.51 = bf16[8,128,512]{2,1,0:T(8,128)(2,1)S(1)} all-to-all(bf16[8,128,512]{2,1,0:T(8,128)(2,1)S(1)} %bitcast.14), channel_id=1, replica_groups=mesh['zl'=4,'co'=2,'x'=4,'zh'=2,'y'=8] {'y'}, dimensions={0} | all-to-all | bytes 2097152 | tf_op jit(solution)/shard_map/all_to_all | solution.py:92
  77.0 0.1 convert_reduce_fusion
  77.1 0.1 fusion.3
  77.2 0.1 tile.11
  77.3 29.1 %all_to_all.52 = bf16[8,128,512]{2,1,0:T(8,128)(2,1)S(1)} all-to-all(bf16[8,128,512]{2,1,0:T(8,128)(2,1)S(1)} %tile.11), channel_id=1, replica_groups=mesh['zl'=4,'co'=2,'x'=4,'zh'=2,'y'=8] {'y'}, dimensions={0} | all-to-all | bytes 2097152 | tf_op jit(solution)/shard_map/all_to_all | solution.py:32
  106.5 2.3 %shard_map.76 = bf16[4,4,2,128,128]{4,3,2,1,0:T(8,128)(2,1)} custom-call(bf16[1024,512]{1,0:T(8,128)(2,1)S(1)} %bitcast.10, bf16[1024,256]{1,0:T(8,128)(2,1)S(1)} %copy-done, bf16[1024,256]{1,0:T(8,128)(2,1)S(1)} %copy-done.1, bf16[1024,256]{1,0:T(8,128)(2,1)S(1)} %collective-permute-done.1.other_gate, bf16[1024,256]{1,0:T(8,128)(2,1)S(1)} %collective-permute-done.2.other_up), custom_call_target="tpu_custom_call" | custom-call | tf_op jit(solution)/shard_map/pallas_call | solution.py:67
  108.8 1.9 %collective-permute-start.4 = (bf16[512,1024]{1,0:T(8,128)(2,1)}, bf16[512,1024]{1,0:T(8,128)(2,1)S(1)}, u32[]{:S(2)}, u32[]{:S(2)}) collective-permute-start(bf16[512,1024]{1,0:T(8,128)(2,1)} %get-tuple-element.16), channel_id=1, source_target_pairs={{0,64},{64,0},{1,65},{65,1},{2,66},{66,2},{3,67},{67,3},{4,68},{68... | collective-permute-start | bytes 3145736 | tf_op jit(solution)/shard_map/ppermute | solution.py:28
  110.7 4.8 %all-to-all-start.4 = ((bf16[4,1024,128]{2,1,0:T(8,128)(2,1)}), bf16[4,1024,128]{2,1,0:T(8,128)(2,1)S(1)}, u32[]{:S(2)}, u32[]{:S(2)}) async-start(bf16[4,1024,128]{2,1,0:T(8,128)(2,1)} %bitcast.5), calls=%async_computation.4 | async-start | bytes 2097152 | tf_op jit(solution)/shard_map/all_to_all | solution.py:105
  115.5 0.8 slice.21
  116.3 1.9 %collective-permute-start.5 = (bf16[512,512]{1,0:T(8,128)(2,1)}, bf16[512,512]{1,0:T(8,128)(2,1)}, u32[]{:S(2)}, u32[]{:S(2)}) collective-permute-start(bf16[512,512]{1,0:T(8,128)(2,1)} %slice.21), channel_id=1, source_target_pairs={{0,64},{64,0},{1,65},{65,1},{2,66},{66,2},{3,67},{67,3},{4,68},{68... | collective-permute-start | bytes 1572872 | tf_op jit(solution)/shard_map/ppermute | solution.py:28
  118.2 0.7 collective-permute-start.3
  118.9 0.0 collective-permute-done.3
  118.9 10.3 %all-to-all-done.4 = bf16[4,1024,128]{2,1,0:T(8,128)(2,1)S(1)} async-done(((bf16[4,1024,128]{2,1,0:T(8,128)(2,1)}), bf16[4,1024,128]{2,1,0:T(8,128)(2,1)S(1)}, u32[]{:S(2)}, u32[]{:S(2)}) %all-to-all-start.4) | async-done | bytes 1048608 | tf_op jit(solution)/shard_map/all_to_all | solution.py:105
  129.2 0.9 reduce_sum.34
  130.1 5.7 %all-to-all-start.5 = ((bf16[8,128,128]{2,1,0:T(8,128)(2,1)}), bf16[8,128,128]{2,1,0:T(8,128)(2,1)S(1)}, u32[]{:S(2)}, u32[]{:S(2)}) async-start(bf16[8,128,128]{2,1,0:T(8,128)(2,1)} %bitcast.6), calls=%async_computation.5 | async-start | bytes 524288 | tf_op jit(solution)/shard_map/all_to_all | solution.py:107
  135.8 0.0 collective-permute-done.4
  135.8 1.8 %fusion.7 = f32[1024,512]{1,0:T(8,128)S(1)} fusion(bf16[512,1024]{1,0:T(8,128)(2,1)S(1)} %collective-permute-done.4, bf16[512,512]{1,0:T(8,128)(2,1)} %collective-permute-done.5), kind=kOutput, calls=%fused_computation.14 | convolution fusion | flops 536870912 | bytes 3670016 | tf_op jit(solution)/shard_map/dot_general | solution.py:112
  137.6 2.0 %add_convert_fusion = bf16[1024,512]{1,0:T(8,128)(2,1)S(1)} fusion(f32[1024,512]{1,0:T(8,128)S(1)} %fusion.7, bf16[512,1024]{1,0:T(8,128)(2,1)} %get-tuple-element.16, bf16[1024,512]{1,0:T(8,128)(2,1)S(1)} %bitcast.12), kind=kOutput, calls=%fused_computation | convolution fusion | flops 537919488 | bytes 4718592 | tf_op jit(solution)/shard_map/dot_general | solution.py:111
  139.6 1.0 fusion.6
  140.6 4.0 %all-to-all-done.5 = bf16[8,128,128]{2,1,0:T(8,128)(2,1)S(1)} async-done(((bf16[8,128,128]{2,1,0:T(8,128)(2,1)}), bf16[8,128,128]{2,1,0:T(8,128)(2,1)S(1)}, u32[]{:S(2)}, u32[]{:S(2)}) %all-to-all-start.5) | async-done | bytes 262176 | tf_op jit(solution)/shard_map/all_to_all | solution.py:107
  144.6 0.7 reduce_sum.35
  145.3 0.6 copy.9
  (10 shorter events, 0.0 us)
Async XLA Ops:
  0.6 25.7 %copy-start = (bf16[1024,256]{1,0:T(8,128)(2,1)S(1)}, bf16[1024,256]{1,0:T(8,128)(2,1)}, u32[]{:S(2)}) copy-start(bf16[1024,256]{1,0:T(8,128)(2,1)} %own_gate.3) | copy-start | bytes 1572868
  0.6 27.7 %copy-start.1 = (bf16[1024,256]{1,0:T(8,128)(2,1)S(1)}, bf16[1024,256]{1,0:T(8,128)(2,1)}, u32[]{:S(2)}) copy-start(bf16[1024,256]{1,0:T(8,128)(2,1)} %own_up.3) | copy-start | bytes 1572868
  0.7 30.1 %copy-start.2 = (bf16[128,256]{1,0:T(8,128)(2,1)S(1)}, bf16[128,256]{1,0:T(8,128)(2,1)}, u32[]{:S(2)}) copy-start(bf16[128,256]{1,0:T(8,128)(2,1)} %param.7) | copy-start | bytes 196612
  21.6 15.8 %all-to-all-start.1 = ((bf16[4,1024,128]{2,1,0:T(8,128)(2,1)}), bf16[4,1024,128]{2,1,0:T(8,128)(2,1)S(1)}, u32[]{:S(2)}, u32[]{:S(2)}) async-start(bf16[4,1024,128]{2,1,0:T(8,128)(2,1)} %tile.10), calls=%async_computation.1 | async-start | bytes 2097152 | tf_op jit(solution)/shard_map/all_to_all | solution.py:32
  26.4 11.0 %collective-permute-start.1 = (bf16[1024,256]{1,0:T(8,128)(2,1)S(1)}, bf16[1024,256]{1,0:T(8,128)(2,1)S(1)}, u32[]{:S(2)}, u32[]{:S(2)}) collective-permute-start(bf16[1024,256]{1,0:T(8,128)(2,1)S(1)} %copy-done), channel_id=1, source_target_pairs={{0,64},{64,0},{1,65},{65,1},{2,66},{66,2},{3,67},{67,3},{4,68},{68... | collective-permute-start | bytes 1572872 | tf_op jit(solution)/shard_map/ppermute | solution.py:28
  28.3 9.1 %collective-permute-start.2 = (bf16[1024,256]{1,0:T(8,128)(2,1)S(1)}, bf16[1024,256]{1,0:T(8,128)(2,1)S(1)}, u32[]{:S(2)}, u32[]{:S(2)}) collective-permute-start(bf16[1024,256]{1,0:T(8,128)(2,1)S(1)} %copy-done.1), channel_id=1, source_target_pairs={{0,64},{64,0},{1,65},{65,1},{2,66},{66,2},{3,67},{67,3},{4,68},{68... | collective-permute-start | bytes 1572872 | tf_op jit(solution)/shard_map/ppermute | solution.py:28
  30.7 0.7 collective-permute-start
  108.8 27.0 %collective-permute-start.4 = (bf16[512,1024]{1,0:T(8,128)(2,1)}, bf16[512,1024]{1,0:T(8,128)(2,1)S(1)}, u32[]{:S(2)}, u32[]{:S(2)}) collective-permute-start(bf16[512,1024]{1,0:T(8,128)(2,1)} %get-tuple-element.16), channel_id=1, source_target_pairs={{0,64},{64,0},{1,65},{65,1},{2,66},{66,2},{3,67},{67,3},{4,68},{68... | collective-permute-start | bytes 3145736 | tf_op jit(solution)/shard_map/ppermute | solution.py:28
  110.7 18.5 %all-to-all-start.4 = ((bf16[4,1024,128]{2,1,0:T(8,128)(2,1)}), bf16[4,1024,128]{2,1,0:T(8,128)(2,1)S(1)}, u32[]{:S(2)}, u32[]{:S(2)}) async-start(bf16[4,1024,128]{2,1,0:T(8,128)(2,1)} %bitcast.5), calls=%async_computation.4 | async-start | bytes 2097152 | tf_op jit(solution)/shard_map/all_to_all | solution.py:105
  116.3 19.4 %collective-permute-start.5 = (bf16[512,512]{1,0:T(8,128)(2,1)}, bf16[512,512]{1,0:T(8,128)(2,1)}, u32[]{:S(2)}, u32[]{:S(2)}) collective-permute-start(bf16[512,512]{1,0:T(8,128)(2,1)} %slice.21), channel_id=1, source_target_pairs={{0,64},{64,0},{1,65},{65,1},{2,66},{66,2},{3,67},{67,3},{4,68},{68... | collective-permute-start | bytes 1572872 | tf_op jit(solution)/shard_map/ppermute | solution.py:28
  118.2 0.7 collective-permute-start.3
  130.1 14.5 %all-to-all-start.5 = ((bf16[8,128,128]{2,1,0:T(8,128)(2,1)}), bf16[8,128,128]{2,1,0:T(8,128)(2,1)S(1)}, u32[]{:S(2)}, u32[]{:S(2)}) async-start(bf16[8,128,128]{2,1,0:T(8,128)(2,1)} %bitcast.6), calls=%async_computation.5 | async-start | bytes 524288 | tf_op jit(solution)/shard_map/all_to_all | solution.py:107

commit v6 on v5

--- a/solution.py
+++ b/solution.py
@@ -99,14 +99,15 @@
     gate_grad = upstream * up_sum * sigmoid_gate * (1.0 + gate_sum * (1.0 - sigmoid_gate))
     up_grad = upstream * activated
     mine = jnp.concatenate([gate_grad.astype(BF16), up_grad.astype(BF16)], axis=1)
+    mine, rows = lax.optimization_barrier((mine, rows))
     grads = spread(mine, "y", 8)
+    grads, other_rows = lax.optimization_barrier((grads, swap_cores(rows)))
     (blocks,) = call(backward_kernel, [(4, 4, 2, 128, 128)], (grads,) + weights)
-    blocks, grads, rows = lax.optimization_barrier((blocks, grads, rows))
+    blocks, grads, hidden = lax.optimization_barrier((blocks, grads, hidden))
     blocks = lax.all_to_all(blocks.reshape(32 * 128, 128), "x", 0, 0, tiled=True)
     blocks = jnp.sum(blocks.reshape(4, 8 * 128, 128).astype(F32), axis=0).astype(BF16)
     blocks = lax.all_to_all(blocks, RING, 0, 0, tiled=True)
     received_grads = swap_cores(grads[512:])
-    other_rows = swap_cores(rows)
     hidden = lax.ppermute(hidden, ("zl", "co", "y"), to_home)
     wgrad = lax.dot_general(rows, grads[:512], ROWS, preferred_element_type=F32)
     wgrad += lax.dot_general(other_rows, received_grads, ROWS, preferred_element_type=F32)

time: 149 us -> 146 us (0.980)
  blocking collectives: 86.2 us -> 57.1 us
  waiting for transfers between devices: 20.3 us -> 40.1 us
  starting transfers between devices: 24.7 us -> 30.3 us
    all_to_all x2 -> x1, blocking collectives: 48.1 us -> 19 us  [spread(): return lax.all_to_all(jnp.tile(value, (count, 1)), axes, 0, 0, tiled=True)]
    all_to_all x1 -> x2, waiting for transfers between devices: 6 us -> 27 us  [spread(): return lax.all_to_all(jnp.tile(value, (count, 1)), axes, 0, 0, tiled=True)]
    all_to_all x1, waiting for transfers between devices: 10.3 us -> 4.4 us  [body(): lax.all_to_all(blocks.reshape(32 * 128, 128), 'x', 0, 0, tiled=True)]
    all_to_all x1 -> x2, starting transfers between devices: 4.77 us -> 8.33 us  [spread(): return lax.all_to_all(jnp.tile(value, (count, 1)), axes, 0, 0, tiled=True)]
    ppermute x4, waiting for transfers between devices: 0.01 us -> 2.98 us  [swap_cores(): return lax.ppermute(value, 'co', [(0, 1), (1, 0)])]
    all_to_all x1, starting transfers between devices: 5.67 us -> 7.62 us  [body(): blocks = lax.all_to_all(blocks, RING, 0, 0, tiled=True)]
    all_to_all x1, waiting for transfers between devices: 4.03 us -> 5.73 us  [body(): blocks = lax.all_to_all(blocks, RING, 0, 0, tiled=True)]
  transfers between devices with their start and end apart: 9 -> 10, of which waited for: 3 -> 5; matrix products, arithmetic and copies ran while one was open for 4% -> 5% of each run, Pallas kernels for 0% -> 0%
where the time goes in v6:
time: 146 us; the launch traced here: 144 us
  blocking collectives  57.1 us (39%)
  waiting for transfers between devices  40.1 us (27%)
  starting transfers between devices  30.3 us (21%)
  local copies, waits for them, and re-layouts  5.59 us (4%)
  matrix products  4.91 us (3%)
  Pallas kernels  3.54 us (2%)
  other arithmetic  1.8 us (1%)
    all_to_all x1, blocking collectives, body(): parts = lax.all_to_all(parts, 'y', 0, 0, tiled=True)  38.1 us
    all_to_all x2, waiting for transfers between devices, spread(): return lax.all_to_all(jnp.tile(value, (count, 1)), axes, 0, 0, tiled=True)  27 us
    all_to_all x1, blocking collectives, spread(): return lax.all_to_all(jnp.tile(value, (count, 1)), axes, 0, 0, tiled=True)  19 us
    all_to_all x2, starting transfers between devices, spread(): return lax.all_to_all(jnp.tile(value, (count, 1)), axes, 0, 0, tiled=True)  8.33 us
    ppermute x4, starting transfers between devices, swap_cores(): return lax.ppermute(value, 'co', [(0, 1), (1, 0)])  8.15 us
    all_to_all x1, starting transfers between devices, body(): blocks = lax.all_to_all(blocks, RING, 0, 0, tiled=True)  7.62 us
    all_to_all x1, waiting for transfers between devices, body(): blocks = lax.all_to_all(blocks, RING, 0, 0, tiled=True)  5.73 us
    all_to_all x1, starting transfers between devices, body(): lax.all_to_all(blocks.reshape(32 * 128, 128), 'x', 0, 0, tiled=True)  4.93 us
  transfers between devices with their start and end apart: 10, of which 5 were waited for; matrix products, arithmetic and copies ran while one was open for 5% of the time, Pallas kernels for 0%

profile of v6, /device:TPU:6, one launch (start us, length us, event | category | flops | bytes accessed | tf_op | source)
XLA Modules:
  0.0 144.1 jit_solution(3964306059072942591)
XLA Ops:
  0.7 0.9 tile.8
  1.5 19.0 %all_to_all.51 = bf16[8,128,128]{2,1,0:T(8,128)(2,1)S(1)} all-to-all(bf16[8,128,128]{2,1,0:T(8,128)(2,1)S(1)} %tile.8), channel_id=1, replica_groups=mesh['zl'=4,'co'=2,'x'=4,'zh'=2,'y'=8] {'zl','zh'}, dimensions={0} | all-to-all | bytes 524288 | tf_op jit(solution)/shard_map/all_to_all | solution.py:32
  20.5 1.1 tile.10
  21.6 4.8 %all-to-all-start.1 = ((bf16[4,1024,128]{2,1,0:T(8,128)(2,1)}), bf16[4,1024,128]{2,1,0:T(8,128)(2,1)S(1)}, u32[]{:S(2)}, u32[]{:S(2)}) async-start(bf16[4,1024,128]{2,1,0:T(8,128)(2,1)} %tile.10), calls=%async_computation.1 | async-start | bytes 2097152 | tf_op jit(solution)/shard_map/all_to_all | solution.py:32
  26.4 1.9 %collective-permute-start.1 = (bf16[1024,256]{1,0:T(8,128)(2,1)S(1)}, bf16[1024,256]{1,0:T(8,128)(2,1)S(1)}, u32[]{:S(2)}, u32[]{:S(2)}) collective-permute-start(bf16[1024,256]{1,0:T(8,128)(2,1)S(1)} %copy-done), channel_id=1, source_target_pairs={{0,64},{64,0},{1,65},{65,1},{2,66},{66,2},{3,67},{67,3},{4,68},{68... | collective-permute-start | bytes 1572872 | tf_op jit(solution)/shard_map/ppermute | solution.py:28
  28.3 2.4 %collective-permute-start.2 = (bf16[1024,256]{1,0:T(8,128)(2,1)S(1)}, bf16[1024,256]{1,0:T(8,128)(2,1)S(1)}, u32[]{:S(2)}, u32[]{:S(2)}) collective-permute-start(bf16[1024,256]{1,0:T(8,128)(2,1)S(1)} %copy-done.1), channel_id=1, source_target_pairs={{0,64},{64,0},{1,65},{65,1},{2,66},{66,2},{3,67},{67,3},{4,68},{68... | collective-permute-start | bytes 1572872 | tf_op jit(solution)/shard_map/ppermute | solution.py:28
  30.7 0.7 collective-permute-start
  31.4 6.0 %all-to-all-done.1 = bf16[4,1024,128]{2,1,0:T(8,128)(2,1)S(1)} async-done(((bf16[4,1024,128]{2,1,0:T(8,128)(2,1)}), bf16[4,1024,128]{2,1,0:T(8,128)(2,1)S(1)}, u32[]{:S(2)}, u32[]{:S(2)}) %all-to-all-start.1) | async-done | bytes 1048608 | tf_op jit(solution)/shard_map/all_to_all | solution.py:32
  37.4 1.3 shard_map.75
  38.7 38.1 %all_to_all.52 = bf16[8,128,512]{2,1,0:T(8,128)(2,1)S(1)} all-to-all(bf16[8,128,512]{2,1,0:T(8,128)(2,1)S(1)} %bitcast.14), channel_id=1, replica_groups=mesh['zl'=4,'co'=2,'x'=4,'zh'=2,'y'=8] {'y'}, dimensions={0} | all-to-all | bytes 2097152 | tf_op jit(solution)/shard_map/all_to_all | solution.py:92
  76.8 0.1 convert_reduce_fusion
  77.0 0.1 fusion.4
  77.1 1.1 tile.11
  78.2 3.6 %all-to-all-start.3 = ((bf16[8,128,512]{2,1,0:T(8,128)(2,1)}), bf16[8,128,512]{2,1,0:T(8,128)(2,1)S(1)}, u32[]{:S(2)}, u32[]{:S(2)}) async-start(bf16[8,128,512]{2,1,0:T(8,128)(2,1)} %tile.11), calls=%async_computation.3 | async-start | bytes 2097152 | tf_op jit(solution)/shard_map/all_to_all | solution.py:32
  81.7 1.9 %collective-permute-start.3 = (bf16[512,1024]{1,0:T(8,128)(2,1)}, bf16[512,1024]{1,0:T(8,128)(2,1)}, u32[]{:S(2)}, u32[]{:S(2)}) collective-permute-start(bf16[512,1024]{1,0:T(8,128)(2,1)} %copy-done.2), channel_id=1, source_target_pairs={{0,64},{64,0},{1,65},{65,1},{2,66},{66,2},{3,67},{67,3},{4,68},{68... | collective-permute-start | bytes 3145736 | tf_op jit(solution)/shard_map/ppermute | solution.py:28
  83.7 3.0 %collective-permute-done.3 = bf16[512,1024]{1,0:T(8,128)(2,1)} collective-permute-done((bf16[512,1024]{1,0:T(8,128)(2,1)}, bf16[512,1024]{1,0:T(8,128)(2,1)}, u32[]{:S(2)}, u32[]{:S(2)}) %collective-permute-start.3) | collective-permute-done | bytes 1048608 | tf_op jit(solution)/shard_map/ppermute | solution.py:28
  86.6 21.0 %all-to-all-done.3 = bf16[8,128,512]{2,1,0:T(8,128)(2,1)S(1)} async-done(((bf16[8,128,512]{2,1,0:T(8,128)(2,1)}), bf16[8,128,512]{2,1,0:T(8,128)(2,1)S(1)}, u32[]{:S(2)}, u32[]{:S(2)}) %all-to-all-start.3) | async-done | bytes 1048608 | tf_op jit(solution)/shard_map/all_to_all | solution.py:32
  107.6 2.3 %shard_map.76 = bf16[4,4,2,128,128]{4,3,2,1,0:T(8,128)(2,1)} custom-call(bf16[1024,512]{1,0:T(8,128)(2,1)S(1)} %bitcast.10, bf16[1024,256]{1,0:T(8,128)(2,1)S(1)} %copy-done, bf16[1024,256]{1,0:T(8,128)(2,1)S(1)} %copy-done.1, bf16[1024,256]{1,0:T(8,128)(2,1)S(1)} %collective-permute-done.1.other_gate, bf16[1024,256]{1,0:T(8,128)(2,1)S(1)} %collective-permute-done.2.other_up), custom_call_target="tpu_custom_call" | custom-call | tf_op jit(solution)/shard_map/pallas_call | solution.py:67
  109.9 4.9 %all-to-all-start.4 = ((bf16[4,1024,128]{2,1,0:T(8,128)(2,1)}), bf16[4,1024,128]{2,1,0:T(8,128)(2,1)S(1)}, u32[]{:S(2)}, u32[]{:S(2)}) async-start(bf16[4,1024,128]{2,1,0:T(8,128)(2,1)} %bitcast.5), calls=%async_computation.4 | async-start | bytes 2097152 | tf_op jit(solution)/shard_map/all_to_all | solution.py:107
  114.8 0.8 slice.21
  115.6 1.9 %collective-permute-start.5 = (bf16[512,512]{1,0:T(8,128)(2,1)}, bf16[512,512]{1,0:T(8,128)(2,1)}, u32[]{:S(2)}, u32[]{:S(2)}) collective-permute-start(bf16[512,512]{1,0:T(8,128)(2,1)} %slice.21), channel_id=1, source_target_pairs={{0,64},{64,0},{1,65},{65,1},{2,66},{66,2},{3,67},{67,3},{4,68},{68... | collective-permute-start | bytes 1572872 | tf_op jit(solution)/shard_map/ppermute | solution.py:28
  117.5 0.7 collective-permute-start.4
  118.2 2.1 %fusion = f32[1024,512]{1,0:T(8,128)} fusion(bf16[512,1024]{1,0:T(8,128)(2,1)S(1)} %copy-done.3, bf16[1024,512]{1,0:T(8,128)(2,1)S(1)} %bitcast.12), kind=kOutput, calls=%fused_computation.2 | convolution fusion | flops 536870912 | bytes 3670016 | tf_op jit(solution)/shard_map/dot_general | solution.py:112
  120.3 0.0 collective-permute-done.4
  120.3 4.4 %all-to-all-done.4 = bf16[4,1024,128]{2,1,0:T(8,128)(2,1)S(1)} async-done(((bf16[4,1024,128]{2,1,0:T(8,128)(2,1)}), bf16[4,1024,128]{2,1,0:T(8,128)(2,1)S(1)}, u32[]{:S(2)}, u32[]{:S(2)}) %all-to-all-start.4) | async-done | bytes 1048608 | tf_op jit(solution)/shard_map/all_to_all | solution.py:107
  124.7 0.9 reduce_sum.34
  125.6 7.6 %all-to-all-start.5 = ((bf16[8,128,128]{2,1,0:T(8,128)(2,1)}), bf16[8,128,128]{2,1,0:T(8,128)(2,1)S(1)}, u32[]{:S(2)}, u32[]{:S(2)}) async-start(bf16[8,128,128]{2,1,0:T(8,128)(2,1)} %bitcast.6), calls=%async_computation.5 | async-start | bytes 524288 | tf_op jit(solution)/shard_map/all_to_all | solution.py:109
  133.2 2.8 %add_convert_fusion = bf16[1024,512]{1,0:T(8,128)(2,1)S(1)} fusion(f32[1024,512]{1,0:T(8,128)} %fusion, bf16[512,1024]{1,0:T(8,128)(2,1)} %collective-permute-done.3, bf16[512,512]{1,0:T(8,128)(2,1)} %collective-permute-done.5), kind=kOutput, calls=%fused_computation | convolution fusion | flops 537919488 | bytes 4718592 | tf_op jit(solution)/shard_map/dot_general | solution.py:113
  136.1 1.0 fusion.7
  137.1 5.7 %all-to-all-done.5 = bf16[8,128,128]{2,1,0:T(8,128)(2,1)S(1)} async-done(((bf16[8,128,128]{2,1,0:T(8,128)(2,1)}), bf16[8,128,128]{2,1,0:T(8,128)(2,1)S(1)}, u32[]{:S(2)}, u32[]{:S(2)}) %all-to-all-start.5) | async-done | bytes 262176 | tf_op jit(solution)/shard_map/all_to_all | solution.py:109
  142.8 0.7 reduce_sum.35
  143.5 0.6 copy.9
  (15 shorter events, 0.0 us)
Async XLA Ops:
  0.6 25.8 %copy-start = (bf16[1024,256]{1,0:T(8,128)(2,1)S(1)}, bf16[1024,256]{1,0:T(8,128)(2,1)}, u32[]{:S(2)}) copy-start(bf16[1024,256]{1,0:T(8,128)(2,1)} %own_gate.3) | copy-start | bytes 1572868
  0.6 27.7 %copy-start.1 = (bf16[1024,256]{1,0:T(8,128)(2,1)S(1)}, bf16[1024,256]{1,0:T(8,128)(2,1)}, u32[]{:S(2)}) copy-start(bf16[1024,256]{1,0:T(8,128)(2,1)} %own_up.3) | copy-start | bytes 1572868
  0.7 30.1 %copy-start.4 = (bf16[128,256]{1,0:T(8,128)(2,1)S(1)}, bf16[128,256]{1,0:T(8,128)(2,1)}, u32[]{:S(2)}) copy-start(bf16[128,256]{1,0:T(8,128)(2,1)} %param.7) | copy-start | bytes 196612
  21.6 15.8 %all-to-all-start.1 = ((bf16[4,1024,128]{2,1,0:T(8,128)(2,1)}), bf16[4,1024,128]{2,1,0:T(8,128)(2,1)S(1)}, u32[]{:S(2)}, u32[]{:S(2)}) async-start(bf16[4,1024,128]{2,1,0:T(8,128)(2,1)} %tile.10), calls=%async_computation.1 | async-start | bytes 2097152 | tf_op jit(solution)/shard_map/all_to_all | solution.py:32
  26.4 11.0 %collective-permute-start.1 = (bf16[1024,256]{1,0:T(8,128)(2,1)S(1)}, bf16[1024,256]{1,0:T(8,128)(2,1)S(1)}, u32[]{:S(2)}, u32[]{:S(2)}) collective-permute-start(bf16[1024,256]{1,0:T(8,128)(2,1)S(1)} %copy-done), channel_id=1, source_target_pairs={{0,64},{64,0},{1,65},{65,1},{2,66},{66,2},{3,67},{67,3},{4,68},{68... | collective-permute-start | bytes 1572872 | tf_op jit(solution)/shard_map/ppermute | solution.py:28
  28.3 9.1 %collective-permute-start.2 = (bf16[1024,256]{1,0:T(8,128)(2,1)S(1)}, bf16[1024,256]{1,0:T(8,128)(2,1)S(1)}, u32[]{:S(2)}, u32[]{:S(2)}) collective-permute-start(bf16[1024,256]{1,0:T(8,128)(2,1)S(1)} %copy-done.1), channel_id=1, source_target_pairs={{0,64},{64,0},{1,65},{65,1},{2,66},{66,2},{3,67},{67,3},{4,68},{68... | collective-permute-start | bytes 1572872 | tf_op jit(solution)/shard_map/ppermute | solution.py:28
  30.7 0.7 collective-permute-start
  38.7 38.4 %copy-start.2 = (bf16[512,1024]{1,0:T(8,128)(2,1)}, bf16[512,1024]{1,0:T(8,128)(2,1)S(1)}, u32[]{:S(2)}) copy-start(bf16[512,1024]{1,0:T(8,128)(2,1)S(1)} %get-tuple-element.20) | copy-start | bytes 3145732
  78.2 29.4 %all-to-all-start.3 = ((bf16[8,128,512]{2,1,0:T(8,128)(2,1)}), bf16[8,128,512]{2,1,0:T(8,128)(2,1)S(1)}, u32[]{:S(2)}, u32[]{:S(2)}) async-start(bf16[8,128,512]{2,1,0:T(8,128)(2,1)} %tile.11), calls=%async_computation.3 | async-start | bytes 2097152 | tf_op jit(solution)/shard_map/all_to_all | solution.py:32
  81.7 4.9 %collective-permute-start.3 = (bf16[512,1024]{1,0:T(8,128)(2,1)}, bf16[512,1024]{1,0:T(8,128)(2,1)}, u32[]{:S(2)}, u32[]{:S(2)}) collective-permute-start(bf16[512,1024]{1,0:T(8,128)(2,1)} %copy-done.2), channel_id=1, source_target_pairs={{0,64},{64,0},{1,65},{65,1},{2,66},{66,2},{3,67},{67,3},{4,68},{68... | collective-permute-start | bytes 3145736 | tf_op jit(solution)/shard_map/ppermute | solution.py:28
  109.9 8.4 %copy-start.3 = (bf16[512,1024]{1,0:T(8,128)(2,1)S(1)}, bf16[512,1024]{1,0:T(8,128)(2,1)}, u32[]{:S(2)}) copy-start(bf16[512,1024]{1,0:T(8,128)(2,1)} %copy-done.2) | copy-start | bytes 3145732
  109.9 14.8 %all-to-all-start.4 = ((bf16[4,1024,128]{2,1,0:T(8,128)(2,1)}), bf16[4,1024,128]{2,1,0:T(8,128)(2,1)S(1)}, u32[]{:S(2)}, u32[]{:S(2)}) async-start(bf16[4,1024,128]{2,1,0:T(8,128)(2,1)} %bitcast.5), calls=%async_computation.4 | async-start | bytes 2097152 | tf_op jit(solution)/shard_map/all_to_all | solution.py:107
  115.6 17.6 %collective-permute-start.5 = (bf16[512,512]{1,0:T(8,128)(2,1)}, bf16[512,512]{1,0:T(8,128)(2,1)}, u32[]{:S(2)}, u32[]{:S(2)}) collective-permute-start(bf16[512,512]{1,0:T(8,128)(2,1)} %slice.21), channel_id=1, source_target_pairs={{0,64},{64,0},{1,65},{65,1},{2,66},{66,2},{3,67},{67,3},{4,68},{68... | collective-permute-start | bytes 1572872 | tf_op jit(solution)/shard_map/ppermute | solution.py:28
  117.5 2.8 %collective-permute-start.4 = (bf16[128,256]{1,0:T(8,128)(2,1)S(1)}, bf16[128,256]{1,0:T(8,128)(2,1)S(1)}, u32[]{:S(2)}, u32[]{:S(2)}) collective-permute-start(bf16[128,256]{1,0:T(8,128)(2,1)S(1)} %get-tuple-element.22), channel_id=1, source_target_pairs={{0,0},{1,128},{2,256},{3,384},{4,1},{5,129},{6,257},{7,385},{64,65... | collective-permute-start | bytes 196616 | tf_op jit(solution)/shard_map/ppermute | solution.py:111
  125.6 17.2 %all-to-all-start.5 = ((bf16[8,128,128]{2,1,0:T(8,128)(2,1)}), bf16[8,128,128]{2,1,0:T(8,128)(2,1)S(1)}, u32[]{:S(2)}, u32[]{:S(2)}) async-start(bf16[8,128,128]{2,1,0:T(8,128)(2,1)} %bitcast.6), calls=%async_computation.5 | async-start | bytes 524288 | tf_op jit(solution)/shard_map/all_to_all | solution.py:109
